TPU v7x, 128 devices: a whole 4x4x4 slice. The times are simulated.
128 devices in a mesh: depth: 8 (over x_hi, y), res: 16 (over x_lo, z, core).
Axes of the slice: x: 4 (x_hi: 2, x_lo: 2; x = x_hi * 2 + x_lo), y: 4, z: 4, core: 2. Of those that a mesh axis runs over, the one named last changes fastest.
Arguments:
- family_activity: bfloat16 [2048, 16, 768], P('depth', 'res'), may hold values from -6 to 6
- rescale_factor: float32 [768], replicated, may hold values from 0.25 to 1.75
- asking_weights: bfloat16 [768, 768], P(('depth', 'res')), may hold values from -1.203125 to 1.203125
- lookup_weights: bfloat16 [768, 768], P(('depth', 'res')), may hold values from -1.203125 to 1.203125
- payload_weights: bfloat16 [768, 768], P(('depth', 'res')), may hold values from -0.21875 to 0.21875
- exit_weights: bfloat16 [768, 768], P(('depth', 'res')), may hold values from -0.625 to 0.625
- upstream_adjoint: bfloat16 [2048, 16, 768], P('depth', 'res'), may hold values from -6 to 6
Outputs:
- final_result: bfloat16 [2048, 16, 768], P('depth', 'res')
- alignment_gradient: bfloat16 [2048, 16, 768], P('depth', 'res')
- query_gradient: float32 [768, 768], P(('depth', 'res'))
- key_gradient: float32 [768, 768], P(('depth', 'res'))
- value_gradient: float32 [768, 768], P(('depth', 'res'))
- output_gradient: float32 [768, 768], P(('depth', 'res'))
- gain_gradient: float32 [768], P(('depth', 'res'))
All inputs are finite; a program needn't handle non-finite values.
Results may differ from a plain program's by a relative error of at most 0.022.
The roundings to bfloat16 on the way count: a program that leaves them out, or rounds other values in their place, can miss the bound.
Values may be sent and summed in bfloat16 or wider, within the bound.
A program may use at most 128 MiB of HBM per device.

v0:
```python
import jax
import jax.numpy as jnp
from jax import lax
from jax.sharding import PartitionSpec as P

HEADS = 12
HEAD_DIM = 64


def standardize_entries(family_activity, rescale_factor):
    payload_entries = family_activity.astype(jnp.float32)
    centered = payload_entries - jnp.mean(payload_entries, axis=-1, keepdims=True)
    reciprocal_spread = lax.rsqrt(jnp.mean(centered * centered, axis=-1, keepdims=True) + 1e-05)
    standardized_entries = centered * reciprocal_spread
    return (
        (standardized_entries * rescale_factor).astype(jnp.bfloat16),
        standardized_entries,
        reciprocal_spread,
    )


def project(rows, weight, factor):
    return (factor * jnp.dot(rows, weight, preferred_element_type=jnp.float32)).astype(jnp.bfloat16)


def to_heads(array):
    count, cols = (array.shape[0], array.shape[1])
    return jnp.transpose(array.reshape(count, cols, HEADS, HEAD_DIM), (1, 2, 0, 3)).reshape(
        cols * HEADS, count, HEAD_DIM
    )


def from_heads(array, cols):
    count = array.shape[1]
    return jnp.transpose(array.reshape(cols, HEADS, count, HEAD_DIM), (2, 0, 1, 3)).reshape(
        count, cols, HEADS * HEAD_DIM
    )


def head_pass(query, keys, payload_entries, d_att):
    scale = HEAD_DIM ** (-0.5)
    scores = jnp.dot(query, keys.T, preferred_element_type=jnp.float32)
    probs = jax.nn.softmax(scores, axis=-1)
    probs_b = probs.astype(jnp.bfloat16)
    mixed_homologs = jnp.dot(probs_b, payload_entries, preferred_element_type=jnp.float32).astype(
        jnp.bfloat16
    )
    d_probs = jnp.dot(d_att, payload_entries.T, preferred_element_type=jnp.float32)
    d_scores = probs * (d_probs - jnp.sum(probs * d_probs, axis=-1, keepdims=True))
    d_scores_b = d_scores.astype(jnp.bfloat16)
    d_query = (scale * jnp.dot(d_scores_b, keys, preferred_element_type=jnp.float32)).astype(
        jnp.bfloat16
    )
    key_part = jnp.einsum("st,sd->td", d_scores_b, query, preferred_element_type=jnp.float32)
    value_part = jnp.einsum("st,sd->td", probs_b, d_att, preferred_element_type=jnp.float32)
    return (mixed_homologs, d_query, key_part, value_part)


def body(
    family_activity,
    rescale_factor,
    asking_weights,
    lookup_weights,
    payload_weights,
    exit_weights,
    upstream_adjoint,
):
    query_weight, key_weight, value_weight, output_matrix = (
        lax.all_gather(asking_weights, ("depth", "res"), axis=0, tiled=True),
        lax.all_gather(lookup_weights, ("depth", "res"), axis=0, tiled=True),
        lax.all_gather(payload_weights, ("depth", "res"), axis=0, tiled=True),
        lax.all_gather(exit_weights, ("depth", "res"), axis=0, tiled=True),
    )
    homologs_each_shard, positions_each_shard, embed_span = family_activity.shape
    standardized_source, standardized_entries, reciprocal_spread = standardize_entries(
        family_activity, rescale_factor
    )
    query = project(standardized_source, query_weight, HEAD_DIM ** (-0.5))
    keys = project(standardized_source, key_weight, 1.0)
    payload_entries = project(standardized_source, value_weight, 1.0)
    keys_all, values_all = (
        lax.all_gather(keys, "depth", axis=0, tiled=True),
        lax.all_gather(payload_entries, "depth", axis=0, tiled=True),
    )
    d_att = jnp.dot(upstream_adjoint, output_matrix.T, preferred_element_type=jnp.float32).astype(
        jnp.bfloat16
    )

    def per_head(items):
        return head_pass(items[0], items[1], items[2], items[3])

    mixed_homologs, d_query, key_part, value_part = lax.map(
        per_head, (to_heads(query), to_heads(keys_all), to_heads(values_all), to_heads(d_att))
    )
    mixed_homologs = from_heads(mixed_homologs, positions_each_shard)
    d_query = from_heads(d_query, positions_each_shard)
    key_part = from_heads(key_part, positions_each_shard)
    value_part = from_heads(value_part, positions_each_shard)
    rows = homologs_each_shard * positions_each_shard
    normed_rows = standardized_source.reshape(rows, embed_span)
    part_query = jnp.dot(
        normed_rows.T, d_query.reshape(rows, embed_span), preferred_element_type=jnp.float32
    )
    part_out = jnp.dot(
        mixed_homologs.reshape(rows, embed_span).T,
        upstream_adjoint.reshape(rows, embed_span),
        preferred_element_type=jnp.float32,
    )
    stacked = jnp.stack([key_part, value_part], axis=2).astype(jnp.bfloat16)
    summed = (
        lax.psum_scatter(stacked, "depth", scatter_dimension=0, tiled=True)
        .astype(jnp.float32)
        .astype(jnp.bfloat16)
    )
    d_keys = summed[:, :, 0, :]
    d_values = summed[:, :, 1, :]
    final_result = (
        family_activity.astype(jnp.float32)
        + jnp.dot(mixed_homologs, output_matrix, preferred_element_type=jnp.float32)
    ).astype(jnp.bfloat16)
    part_key = jnp.dot(
        normed_rows.T, d_keys.reshape(rows, embed_span), preferred_element_type=jnp.float32
    )
    part_value = jnp.dot(
        normed_rows.T, d_values.reshape(rows, embed_span), preferred_element_type=jnp.float32
    )
    d_normed = jnp.dot(d_query, query_weight.T, preferred_element_type=jnp.float32)
    d_normed = d_normed + jnp.dot(d_keys, key_weight.T, preferred_element_type=jnp.float32)
    d_normed = d_normed + jnp.dot(d_values, value_weight.T, preferred_element_type=jnp.float32)
    part_gain = jnp.sum((d_normed * standardized_entries).reshape(rows, embed_span), axis=0)
    unit_gradient = d_normed * rescale_factor
    alignment_gradient = upstream_adjoint.astype(jnp.float32) + reciprocal_spread * (
        unit_gradient
        - jnp.mean(unit_gradient, axis=-1, keepdims=True)
        - standardized_entries
        * jnp.mean(unit_gradient * standardized_entries, axis=-1, keepdims=True)
    )
    query_gradient, key_gradient, value_gradient, output_gradient, gain_gradient = (
        lax.psum_scatter(part_query, ("depth", "res"), scatter_dimension=0, tiled=True),
        lax.psum_scatter(part_key, ("depth", "res"), scatter_dimension=0, tiled=True),
        lax.psum_scatter(part_value, ("depth", "res"), scatter_dimension=0, tiled=True),
        lax.psum_scatter(part_out, ("depth", "res"), scatter_dimension=0, tiled=True),
        lax.psum_scatter(part_gain, ("depth", "res"), scatter_dimension=0, tiled=True),
    )
    return (
        final_result,
        alignment_gradient.astype(jnp.bfloat16),
        query_gradient,
        key_gradient,
        value_gradient,
        output_gradient,
        gain_gradient,
    )


def solution(mesh):
    return jax.shard_map(
        body,
        mesh=mesh,
        in_specs=(
            P("depth", "res", None),
            P(),
            P(("depth", "res"), None),
            P(("depth", "res"), None),
            P(("depth", "res"), None),
            P(("depth", "res"), None),
            P("depth", "res", None),
        ),
        out_specs=(
            P("depth", "res", None),
            P("depth", "res", None),
            P(("depth", "res"), None),
            P(("depth", "res"), None),
            P(("depth", "res"), None),
            P(("depth", "res"), None),
            P(("depth", "res")),
        ),
        check_vma=False,
    )
```

profile of v0, /device:TPU:0, one launch (start us, length us, event | category | flops | bytes accessed | tf_op | source)
XLA Modules:
  0.0 2008.5 jit_solution(16909844632739122919)
XLA Ops:
  12.4 193.4 %all-gather.19.cloned.1.call-done = bf16[128,6,768]{2,1,0:T(8,128)(2,1)} async-done(((bf16[1,6,768]{2,1,0:T(8,128)(2,1)}), bf16[128,6,768]{2,1,0:T(8,128)(2,1)}) %all-gather.19.cloned.1.call-update) | async-done | bytes 1179664 | tf_op jit(solution)/shard_map/all_gather | solution.py:70
  209.6 190.0 %all-gather.21.cloned.1.call-done = bf16[128,6,768]{2,1,0:T(8,128)(2,1)} async-done(((bf16[1,6,768]{2,1,0:T(8,128)(2,1)}), bf16[128,6,768]{2,1,0:T(8,128)(2,1)}) %all-gather.21.cloned.1.call-update) | async-done | bytes 1179664 | tf_op jit(solution)/shard_map/all_gather | solution.py:71
  403.3 189.9 %all-gather.17.cloned.1.call-done = bf16[128,6,768]{2,1,0:T(8,128)(2,1)} async-done(((bf16[1,6,768]{2,1,0:T(8,128)(2,1)}), bf16[128,6,768]{2,1,0:T(8,128)(2,1)}) %all-gather.17.cloned.1.call-update) | async-done | bytes 1179664 | tf_op jit(solution)/shard_map/all_gather | solution.py:69
  597.0 189.7 %all-gather.23.cloned.1.call-done = bf16[128,6,768]{2,1,0:T(8,128)(2,1)} async-done(((bf16[1,6,768]{2,1,0:T(8,128)(2,1)}), bf16[128,6,768]{2,1,0:T(8,128)(2,1)}) %all-gather.23.cloned.1.call-update) | async-done | bytes 1179664 | tf_op jit(solution)/shard_map/all_gather | solution.py:72
  790.5 59.3 %all-gather.13.cloned.1.call-done = bf16[2048,768]{1,0:T(8,128)(2,1)} async-done(((bf16[256,768]{1,0:T(8,128)(2,1)}), bf16[2048,768]{1,0:T(8,128)(2,1)}) %all-gather.13.cloned.1.call-update) | async-done | bytes 3145744 | tf_op jit(solution)/shard_map/all_gather | solution.py:82
  853.0 59.5 %all-gather.15.cloned.1.call-done = bf16[2048,768]{1,0:T(8,128)(2,1)} async-done(((bf16[256,768]{1,0:T(8,128)(2,1)}), bf16[2048,768]{1,0:T(8,128)(2,1)}) %all-gather.15.cloned.1.call-update) | async-done | bytes 3145744 | tf_op jit(solution)/shard_map/all_gather | solution.py:83
  912.4 4.7 copy.28
  917.2 132.1 %while.16 = (s32[]{:T(128)}, bf16[12,256,64]{1,2,0:T(8,128)(2,1)}, bf16[12,256,64]{1,2,0:T(8,128)(2,1)}, bf16[12,2048,64]{1,2,0:T(8,128)(2,1)}, bf16[12,2048,64]...) while((s32[]{:T(128)}, bf16[12,256,64]{1,2,0:T(8,128)(2,1)}, ...), condition=%wide.region_6.7_spmd, body=%wide.region_2.6_spmd.sunk | while | flops 412138752 | bytes 22236260 | solution.py:92
  1049.3 6.1 pad_maximum_fusion
  1059.8 91.9 %reduce-scatter.10.cloned.1.call-done = bf16[256,1,2,768]{0,3,2,1:T(8,128)(2,1)} async-done(((bf16[2048,1,2,768]{0,3,2,1:T(8,128)(2,1)}), bf16[256,1,2,768]{0,3,2,1:T(8,128)(2,1)}) %reduce-scatter.10.cloned.1.call-update) | async-done | bytes 786448 | tf_op jit(solution)/shard_map/reduce_scatter | solution.py:111
  1157.0 365.5 %fusion.71 = (f32[8,768]{1,0:T(8,128)}, f32[8,768]{1,0:T(8,128)}, f32[8,768]{1,0:T(8,128)}, f32[8,768]{1,0:T(8,128)}) fusion(f32[768,768]{1,0:T(8,128)} %fusion.66, f32[768,768]{1,0:T(8,128)} %fusion.62, f32[768,768]{1,0:T(8,128)} %fusion.63, f32[768,768]{1,0:T(8,128)S(1)} %fusion.59), kind=kCustom, calls=%all-reduce-scatter.4 | all-reduce-scatter fusion | flops 3145729 | bytes 9535488
  1538.1 10.5 collective-permute-start.104
  1548.5 5.0 collective-permute-start.105
  1555.2 9.9 collective-permute-start.107
  1566.7 6.7 collective-permute-start.109
  1585.6 3.5 collective-permute-start.116
  1598.9 3.4 collective-permute-start.123
  1607.3 3.6 collective-permute-start.96
  1610.9 10.2 collective-permute-start.97
  1621.1 10.2 collective-permute-start.98
  1631.3 4.9 collective-permute-start.99
  1641.0 3.7 collective-permute-start.66
  1644.8 5.1 collective-permute-start.67
  1659.4 3.4 collective-permute-start.71
  1662.8 3.4 collective-permute-start.72
  1666.3 4.1 collective-permute-start.73
  1670.4 4.6 collective-permute-start.74
  1675.0 4.4 collective-permute-start.75
  1679.4 4.0 collective-permute-start.76
  1683.5 5.2 collective-permute-start.77
  1688.8 4.6 collective-permute-start.78
  1700.0 3.7 collective-permute-start.83
  1730.8 3.7 collective-permute-start.34
  1734.5 4.5 collective-permute-start.35
  1754.0 3.4 collective-permute-start.42
  1757.4 4.8 collective-permute-start.43
  1809.1 4.5 collective-permute-start.11
  1816.1 3.6 collective-permute-start.13
  1832.0 3.7 collective-permute-start.2
  1843.2 62.4 %all-reduce.4 = f32[768]{0:T(1024)S(1)} all-reduce(f32[768]{0:T(1024)S(1)} %get-tuple-element.79), channel_id=9, replica_groups=mesh['depth'=8,'res'=16] {'depth','res'}, use_global_device_ids=true, to_apply=%region_15.16.clone | all-reduce | flops 768 | bytes 6144
  1911.8 4.0 collective-permute-start.24
  1915.8 4.6 collective-permute-start.25
  1920.5 5.3 collective-permute-start.26
  1925.8 4.6 collective-permute-start.27
  1931.2 14.6 concatenate.11
  1948.8 4.6 collective-permute-start.3
  1958.8 23.5 %concatenate.10 = f32[262,768]{1,0:T(8,128)S(1)} concatenate(f32[6,768]{1,0:T(8,128)S(1)} %collective-permute-done.63, f32[8,768]{1,0:T(8,128)S(1)} %collective-permute-done.62, f32[8,768]{1,0:T(8,128)S(1)} %collective-permute-done.61, f32[8,768]{1,0:T(8,128)S(1)} %collective-permute-done.60, f32[8,768]{1,0:T(8,128)S(1)} %collective-permute-done.59, f32[8,768]{1,0:T(8,128)} %copy-done.110, ...), dimensions={0} | concatenate | bytes 1609728
  1992.3 3.8 collective-permute-start.9
  (595 shorter events, 371.0 us)
Async XLA Ops:
  7.2 198.7 %all-gather.19.cloned.1.call-start = ((), (), s32[]{:S(2)}) async-start(), calls=%async_computation.5 | async-start | bytes 1585152 | tf_op jit(solution)/shard_map/all_gather | solution.py:70
  7.9 391.6 %all-gather.21.cloned.1.call-start = ((), (), s32[]{:S(2)}) async-start(), calls=%async_computation.6 | async-start | bytes 1585152 | tf_op jit(solution)/shard_map/all_gather | solution.py:71
  8.7 584.5 %all-gather.17.cloned.1.call-start = ((), (), s32[]{:S(2)}) async-start(), calls=%async_computation.4 | async-start | bytes 1585152 | tf_op jit(solution)/shard_map/all_gather | solution.py:69
  9.4 777.3 %all-gather.23.cloned.1.call-start = ((), (), s32[]{:S(2)}) async-start(), calls=%async_computation.7 | async-start | bytes 1585152 | tf_op jit(solution)/shard_map/all_gather | solution.py:72
  10.0 839.8 %all-gather.13.cloned.1.call-start = ((), (), s32[]{:S(2)}) async-start(), calls=%async_computation.2 | async-start | bytes 3538944 | tf_op jit(solution)/shard_map/all_gather | solution.py:82
  209.5 702.9 %all-gather.15.cloned.1.call-start = ((), (), s32[]{:S(2)}) async-start(), calls=%async_computation.3 | async-start | bytes 3538944 | tf_op jit(solution)/shard_map/all_gather | solution.py:83
  403.2 748.6 %reduce-scatter.10.cloned.1.call-start = ((), (), s32[]{:S(2)}) async-start(), calls=%async_computation.1 | async-start | bytes 7077888 | tf_op jit(solution)/shard_map/reduce_scatter | solution.py:111
  1528.7 19.8 collective-permute-start.100
  1530.0 23.5 %collective-permute-start.101 = (f32[8,768]{1,0:T(8,128)}, f32[8,768]{1,0:T(8,128)S(1)}, u32[]{:S(2)}, u32[]{:S(2)}) collective-permute-start(f32[8,768]{1,0:T(8,128)} %get-tuple-element.106), channel_id=1, source_target_pairs={{0,6},{1,7},{2,8},{3,9},{4,10},{5,11},{6,12},{7,13},{8,14},{9,15},... | collective-permute-start | bytes 73736
  1531.3 23.9 %collective-permute-start.102 = (f32[8,768]{1,0:T(8,128)}, f32[8,768]{1,0:T(8,128)S(1)}, u32[]{:S(2)}, u32[]{:S(2)}) collective-permute-start(f32[8,768]{1,0:T(8,128)} %get-tuple-element.106), channel_id=1, source_target_pairs={{0,7},{1,8},{2,9},{3,10},{4,11},{5,12},{6,13},{7,14},{8,15},{9,16}... | collective-permute-start | bytes 73736
  1532.6 32.4 %collective-permute-start.103 = (f32[8,768]{1,0:T(8,128)}, f32[8,768]{1,0:T(8,128)S(1)}, u32[]{:S(2)}, u32[]{:S(2)}) collective-permute-start(f32[8,768]{1,0:T(8,128)} %get-tuple-element.106), channel_id=1, source_target_pairs={{0,8},{1,9},{2,10},{3,11},{4,12},{5,13},{6,14},{7,15},{8,16},{9,17... | collective-permute-start | bytes 73736
  1538.1 28.6 %collective-permute-start.104 = (f32[8,768]{1,0:T(8,128)}, f32[8,768]{1,0:T(8,128)S(1)}, u32[]{:S(2)}, u32[]{:S(2)}) collective-permute-start(f32[8,768]{1,0:T(8,128)} %get-tuple-element.106), channel_id=1, source_target_pairs={{0,9},{1,10},{2,11},{3,12},{4,13},{5,14},{6,15},{7,16},{8,17},{9,1... | collective-permute-start | bytes 73736
  1548.5 24.8 %collective-permute-start.105 = (f32[8,768]{1,0:T(8,128)}, f32[8,768]{1,0:T(8,128)S(1)}, u32[]{:S(2)}, u32[]{:S(2)}) collective-permute-start(f32[8,768]{1,0:T(8,128)} %get-tuple-element.106), channel_id=1, source_target_pairs={{0,10},{1,11},{2,12},{3,13},{4,14},{5,15},{6,16},{7,17},{8,18},{9,... | collective-permute-start | bytes 73736
  1553.5 22.3 %collective-permute-start.106 = (f32[8,768]{1,0:T(8,128)}, f32[8,768]{1,0:T(8,128)S(1)}, u32[]{:S(2)}, u32[]{:S(2)}) collective-permute-start(f32[8,768]{1,0:T(8,128)} %get-tuple-element.106), channel_id=1, source_target_pairs={{0,11},{1,12},{2,13},{3,14},{4,15},{5,16},{6,17},{7,18},{8,19},{9,... | collective-permute-start | bytes 73736
  1555.2 24.1 %collective-permute-start.107 = (f32[8,768]{1,0:T(8,128)}, f32[8,768]{1,0:T(8,128)S(1)}, u32[]{:S(2)}, u32[]{:S(2)}) collective-permute-start(f32[8,768]{1,0:T(8,128)} %get-tuple-element.106), channel_id=1, source_target_pairs={{0,12},{1,13},{2,14},{3,15},{4,16},{5,17},{6,18},{7,19},{8,20},{9,... | collective-permute-start | bytes 73736
  1602.3 18.7 collective-permute-start.124
  1604.0 27.3 %collective-permute-start.125 = (f32[8,768]{1,0:T(8,128)}, f32[8,768]{1,0:T(8,128)S(1)}, u32[]{:S(2)}, u32[]{:S(2)}) collective-permute-start(f32[8,768]{1,0:T(8,128)} %get-tuple-element.106), channel_id=1, source_target_pairs={{0,30},{1,31},{2,32},{3,33},{4,34},{5,35},{6,36},{7,37},{8,38},{9,... | collective-permute-start | bytes 73736
  1606.0 30.3 %collective-permute-start.126 = (f32[8,768]{1,0:T(8,128)}, f32[8,768]{1,0:T(8,128)S(1)}, u32[]{:S(2)}, u32[]{:S(2)}) collective-permute-start(f32[8,768]{1,0:T(8,128)} %get-tuple-element.106), channel_id=1, source_target_pairs={{0,31},{1,32},{2,33},{3,34},{4,35},{5,36},{6,37},{7,38},{8,39},{9,... | collective-permute-start | bytes 73736
  1607.3 30.8 %collective-permute-start.96 = (f32[8,768]{1,0:T(8,128)}, f32[8,768]{1,0:T(8,128)S(1)}, u32[]{:S(2)}, u32[]{:S(2)}) collective-permute-start(f32[8,768]{1,0:T(8,128)} %get-tuple-element.106), channel_id=1, source_target_pairs={{0,1},{1,2},{2,3},{3,4},{4,5},{5,6},{6,7},{7,8},{8,9},{9,10},{10,1... | collective-permute-start | bytes 73736
  1610.9 30.1 %collective-permute-start.97 = (f32[8,768]{1,0:T(8,128)}, f32[8,768]{1,0:T(8,128)S(1)}, u32[]{:S(2)}, u32[]{:S(2)}) collective-permute-start(f32[8,768]{1,0:T(8,128)} %get-tuple-element.106), channel_id=1, source_target_pairs={{0,2},{1,3},{2,4},{3,5},{4,6},{5,7},{6,8},{7,9},{8,10},{9,11},{10,... | collective-permute-start | bytes 73736
  1621.1 23.6 %collective-permute-start.98 = (f32[8,768]{1,0:T(8,128)}, f32[8,768]{1,0:T(8,128)S(1)}, u32[]{:S(2)}, u32[]{:S(2)}) collective-permute-start(f32[8,768]{1,0:T(8,128)} %get-tuple-element.106), channel_id=1, source_target_pairs={{0,3},{1,4},{2,5},{3,6},{4,7},{5,8},{6,9},{7,10},{8,11},{9,12},{10... | collective-permute-start | bytes 73736
  1631.3 18.6 collective-permute-start.99
  1638.1 18.5 collective-permute-start.65
  1641.0 18.4 collective-permute-start.66
  1644.8 18.0 collective-permute-start.67
  1653.2 17.2 collective-permute-start.69
  1656.6 18.4 collective-permute-start.70
  1659.4 20.1 collective-permute-start.71
  1662.8 20.7 %collective-permute-start.72 = (f32[8,768]{1,0:T(8,128)}, f32[8,768]{1,0:T(8,128)S(1)}, u32[]{:S(2)}, u32[]{:S(2)}) collective-permute-start(f32[8,768]{1,0:T(8,128)} %get-tuple-element.105), channel_id=1, source_target_pairs={{0,9},{1,10},{2,11},{3,12},{4,13},{5,14},{6,15},{7,16},{8,17},{9,1... | collective-permute-start | bytes 73736
  1666.3 22.5 %collective-permute-start.73 = (f32[8,768]{1,0:T(8,128)}, f32[8,768]{1,0:T(8,128)S(1)}, u32[]{:S(2)}, u32[]{:S(2)}) collective-permute-start(f32[8,768]{1,0:T(8,128)} %get-tuple-element.105), channel_id=1, source_target_pairs={{0,10},{1,11},{2,12},{3,13},{4,14},{5,15},{6,16},{7,17},{8,18},{9,... | collective-permute-start | bytes 73736
  1670.4 23.0 %collective-permute-start.74 = (f32[8,768]{1,0:T(8,128)}, f32[8,768]{1,0:T(8,128)S(1)}, u32[]{:S(2)}, u32[]{:S(2)}) collective-permute-start(f32[8,768]{1,0:T(8,128)} %get-tuple-element.105), channel_id=1, source_target_pairs={{0,11},{1,12},{2,13},{3,14},{4,15},{5,16},{6,17},{7,18},{8,19},{9,... | collective-permute-start | bytes 73736
  1675.0 20.4 %collective-permute-start.75 = (f32[8,768]{1,0:T(8,128)}, f32[8,768]{1,0:T(8,128)S(1)}, u32[]{:S(2)}, u32[]{:S(2)}) collective-permute-start(f32[8,768]{1,0:T(8,128)} %get-tuple-element.105), channel_id=1, source_target_pairs={{0,12},{1,13},{2,14},{3,15},{4,16},{5,17},{6,18},{7,19},{8,20},{9,... | collective-permute-start | bytes 73736
  1679.4 17.3 collective-permute-start.76
  1828.9 81.0 %collective-permute-start.19 = (f32[8,768]{1,0:T(8,128)S(1)}, f32[8,768]{1,0:T(8,128)S(1)}, u32[]{:S(2)}, u32[]{:S(2)}) collective-permute-start(f32[8,768]{1,0:T(8,128)S(1)} %copy-done.13), channel_id=1, source_target_pairs={{0,20},{1,21},{2,22},{3,23},{4,24},{5,25},{6,26},{7,27},{8,28},{9,... | collective-permute-start | bytes 73736
  1832.0 79.7 %collective-permute-start.2 = (f32[8,768]{1,0:T(8,128)S(1)}, f32[8,768]{1,0:T(8,128)S(1)}, u32[]{:S(2)}, u32[]{:S(2)}) collective-permute-start(f32[8,768]{1,0:T(8,128)S(1)} %copy-done.13), channel_id=1, source_target_pairs={{0,3},{1,4},{2,5},{3,6},{4,7},{5,8},{6,9},{7,10},{8,11},{9,12},{10... | collective-permute-start | bytes 73736
  1835.7 80.1 %collective-permute-start.20 = (f32[8,768]{1,0:T(8,128)S(1)}, f32[8,768]{1,0:T(8,128)S(1)}, u32[]{:S(2)}, u32[]{:S(2)}) collective-permute-start(f32[8,768]{1,0:T(8,128)S(1)} %copy-done.13), channel_id=1, source_target_pairs={{0,21},{1,22},{2,23},{3,24},{4,25},{5,26},{6,27},{7,28},{8,29},{9,... | collective-permute-start | bytes 73736
  1837.9 82.5 %collective-permute-start.21 = (f32[8,768]{1,0:T(8,128)S(1)}, f32[8,768]{1,0:T(8,128)S(1)}, u32[]{:S(2)}, u32[]{:S(2)}) collective-permute-start(f32[8,768]{1,0:T(8,128)S(1)} %copy-done.13), channel_id=1, source_target_pairs={{0,22},{1,23},{2,24},{3,25},{4,26},{5,27},{6,28},{7,29},{8,30},{9,... | collective-permute-start | bytes 73736
  1839.6 86.2 %collective-permute-start.22 = (f32[8,768]{1,0:T(8,128)S(1)}, f32[8,768]{1,0:T(8,128)S(1)}, u32[]{:S(2)}, u32[]{:S(2)}) collective-permute-start(f32[8,768]{1,0:T(8,128)S(1)} %copy-done.13), channel_id=1, source_target_pairs={{0,23},{1,24},{2,25},{3,26},{4,27},{5,28},{6,29},{7,30},{8,31},{9,... | collective-permute-start | bytes 73736
  1909.9 35.9 %collective-permute-start.23 = (f32[8,768]{1,0:T(8,128)S(1)}, f32[8,768]{1,0:T(8,128)S(1)}, u32[]{:S(2)}, u32[]{:S(2)}) collective-permute-start(f32[8,768]{1,0:T(8,128)S(1)} %copy-done.13), channel_id=1, source_target_pairs={{0,24},{1,25},{2,26},{3,27},{4,28},{5,29},{6,30},{7,31},{8,32},{9,... | collective-permute-start | bytes 73736
  1911.8 35.7 %collective-permute-start.24 = (f32[8,768]{1,0:T(8,128)S(1)}, f32[8,768]{1,0:T(8,128)S(1)}, u32[]{:S(2)}, u32[]{:S(2)}) collective-permute-start(f32[8,768]{1,0:T(8,128)S(1)} %copy-done.13), channel_id=1, source_target_pairs={{0,25},{1,26},{2,27},{3,28},{4,29},{5,30},{6,31},{7,32},{8,33},{9,... | collective-permute-start | bytes 73736
  1915.8 33.0 %collective-permute-start.25 = (f32[8,768]{1,0:T(8,128)S(1)}, f32[8,768]{1,0:T(8,128)S(1)}, u32[]{:S(2)}, u32[]{:S(2)}) collective-permute-start(f32[8,768]{1,0:T(8,128)S(1)} %copy-done.13), channel_id=1, source_target_pairs={{0,26},{1,27},{2,28},{3,29},{4,30},{5,31},{6,32},{7,33},{8,34},{9,... | collective-permute-start | bytes 73736
  1920.5 32.9 %collective-permute-start.26 = (f32[8,768]{1,0:T(8,128)S(1)}, f32[8,768]{1,0:T(8,128)S(1)}, u32[]{:S(2)}, u32[]{:S(2)}) collective-permute-start(f32[8,768]{1,0:T(8,128)S(1)} %copy-done.13), channel_id=1, source_target_pairs={{0,27},{1,28},{2,29},{3,30},{4,31},{5,32},{6,33},{7,34},{8,35},{9,... | collective-permute-start | bytes 73736
  1925.8 29.8 %collective-permute-start.27 = (f32[8,768]{1,0:T(8,128)S(1)}, f32[8,768]{1,0:T(8,128)S(1)}, u32[]{:S(2)}, u32[]{:S(2)}) collective-permute-start(f32[8,768]{1,0:T(8,128)S(1)} %copy-done.13), channel_id=1, source_target_pairs={{0,28},{1,29},{2,30},{3,31},{4,32},{5,33},{6,34},{7,35},{8,36},{9,... | collective-permute-start | bytes 73736
  1945.8 36.5 %collective-permute-start.28 = (f32[8,768]{1,0:T(8,128)S(1)}, f32[8,768]{1,0:T(8,128)S(1)}, u32[]{:S(2)}, u32[]{:S(2)}) collective-permute-start(f32[8,768]{1,0:T(8,128)S(1)} %copy-done.13), channel_id=1, source_target_pairs={{0,29},{1,30},{2,31},{3,32},{4,33},{5,34},{6,35},{7,36},{8,37},{9,... | collective-permute-start | bytes 73736
  1947.4 37.4 %collective-permute-start.29 = (f32[8,768]{1,0:T(8,128)S(1)}, f32[8,768]{1,0:T(8,128)S(1)}, u32[]{:S(2)}, u32[]{:S(2)}) collective-permute-start(f32[8,768]{1,0:T(8,128)S(1)} %copy-done.13), channel_id=1, source_target_pairs={{0,30},{1,31},{2,32},{3,33},{4,34},{5,35},{6,36},{7,37},{8,38},{9,... | collective-permute-start | bytes 73736
  1948.8 38.4 %collective-permute-start.3 = (f32[8,768]{1,0:T(8,128)S(1)}, f32[8,768]{1,0:T(8,128)S(1)}, u32[]{:S(2)}, u32[]{:S(2)}) collective-permute-start(f32[8,768]{1,0:T(8,128)S(1)} %copy-done.13), channel_id=1, source_target_pairs={{0,4},{1,5},{2,6},{3,7},{4,8},{5,9},{6,10},{7,11},{8,12},{9,13},{1... | collective-permute-start | bytes 73736
  1953.3 36.0 %collective-permute-start.30 = (f32[8,768]{1,0:T(8,128)S(1)}, f32[8,768]{1,0:T(8,128)S(1)}, u32[]{:S(2)}, u32[]{:S(2)}) collective-permute-start(f32[8,768]{1,0:T(8,128)S(1)} %copy-done.13), channel_id=1, source_target_pairs={{0,31},{1,32},{2,33},{3,34},{4,35},{5,36},{6,37},{7,38},{8,39},{9,... | collective-permute-start | bytes 73736
  1955.6 36.7 %collective-permute-start.4 = (f32[8,768]{1,0:T(8,128)S(1)}, f32[8,768]{1,0:T(8,128)S(1)}, u32[]{:S(2)}, u32[]{:S(2)}) collective-permute-start(f32[8,768]{1,0:T(8,128)S(1)} %copy-done.13), channel_id=1, source_target_pairs={{0,5},{1,6},{2,7},{3,8},{4,9},{5,10},{6,11},{7,12},{8,13},{9,14},{... | collective-permute-start | bytes 73736
  (198 other events, 12003.2 us)
Sparse Core Ops, SparseCore 0:
  9.7 196.0 all-gather.18
  207.6 191.9 all-gather.20
  401.3 191.9 all-gather.16
  594.8 191.9 all-gather.22
  788.9 60.8 all-gather.12
  851.9 60.4 all-gather.14
  1055.5 96.2 reduce-scatter.9
where the time goes:
time: 2020 us; the launch traced here: 2010 us
  waiting for transfers between devices  979 us (48%)
  blocking collectives  428 us (21%)
  starting transfers between devices  354 us (18%)
  matrix products  136 us (7%)
  local copies, waits for them, and re-layouts  71.3 us (4%)
  other arithmetic  22.2 us (1%)
    unnamed x2, blocking collectives  428 us
    unnamed x128, starting transfers between devices  354 us
    all_gather x1, waiting for transfers between devices, body(): lax.all_gather(lookup_weights, ('depth', 'res'), axis=0, tiled=True)  193 us
    all_gather x1, waiting for transfers between devices, body(): lax.all_gather(payload_weights, ('depth', 'res'), axis=0, tiled=True)  190 us
    all_gather x1, waiting for transfers between devices, body(): lax.all_gather(asking_weights, ('depth', 'res'), axis=0, tiled=True)  190 us
    all_gather x1, waiting for transfers between devices, body(): lax.all_gather(exit_weights, ('depth', 'res'), axis=0, tiled=True)  190 us
    reduce_scatter x1, waiting for transfers between devices, body(): lax.psum_scatter(stacked, 'depth', scatter_dimension=0, tiled=True)  91.9 us
    unnamed x239, local copies, waits for them, and re-layouts  61.6 us
  transfers between devices with their start and end apart: 135, of which 9 were waited for; matrix products, arithmetic and copies ran while one was open for 4% of the time, Pallas kernels for 0%

commit v1 on v0

v1 whole, which is shorter than its diff:
```python
import jax
import jax.numpy as jnp
from jax import lax
from jax.experimental import pallas as pl
from jax.experimental.pallas import tpu as pltpu
from jax.sharding import PartitionSpec as P

HEADS = 12
HD = 64
E = 768
ND = 8
NR = 16
ROWS = 256
SEQ = ND * ROWS
SCALE = HD ** (-0.5)
MESH = pl.DeviceIdType.MESH
BF = jnp.bfloat16
F32 = jnp.float32
VMEM_LIMIT = 56 * 1024 * 1024


def place():
    d = lax.axis_index("depth")
    r = lax.axis_index("res")
    return d, r, d // 4, d % 4, r // 8, (r // 2) % 4, r % 2


def at(d, r):
    return {"depth": d, "res": r}


def barrier(peers):
    sem = pltpu.get_barrier_semaphore()
    for peer in peers:
        pl.semaphore_signal(sem, inc=1, device_id=peer, device_id_type=MESH)
    pl.semaphore_wait(sem, len(peers))


def remote(src, dst, send, recv, peer):
    return pltpu.make_async_remote_copy(
        src_ref=src, dst_ref=dst, send_sem=send, recv_sem=recv, device_id=peer, device_id_type=MESH
    )


def dot(a, b, dims):
    return lax.dot_general(a, b, ((dims[0], dims[1]), ((), ())), preferred_element_type=F32)


def gather_kernel(n_ref, u_ref, w_ref, n_all, u_all, w_all, ns, nr, us, ur, ws, wr, loc):
    d, r, xh, y, xl, z, core = place()
    zc = z * 2 + core
    depth_peers = [at((d + s) % ND, r) for s in range(1, ND)]
    y_peers = [at(xh * 4 + (y + s) % 4, r) for s in range(1, 4)]
    x_peers = [at((1 - xh) * 4 + y, r), at(d, (1 - xl) * 8 + zc), at((1 - xh) * 4 + y, (1 - xl) * 8 + zc)]
    z_peers = [at(d, xl * 8 + ((z + s) % 4) * 2 + core) for s in range(1, 4)]
    c_peer = at(d, xl * 8 + z * 2 + 1 - core)
    barrier(depth_peers + x_peers[1:] + z_peers + [c_peer])

    own = [
        pltpu.make_async_copy(n_ref, n_all.at[d], loc.at[0]),
        pltpu.make_async_copy(u_ref, u_all.at[d], loc.at[1]),
        pltpu.make_async_copy(w_ref, w_all.at[xh, y, xl, zc], loc.at[2]),
    ]
    for c in own:
        c.start()
    cy = [remote(w_ref, w_all.at[xh, y, xl, zc], ws.at[s], wr.at[s], y_peers[s]) for s in range(3)]
    for c in cy:
        c.start()
    cn = [remote(n_ref, n_all.at[d], ns.at[s], nr.at[s], depth_peers[s]) for s in range(7)]
    for c in cn:
        c.start()
    own[2].wait()
    for c in cy:
        c.wait()
    slab = w_all.at[xh, :, xl, zc]
    cx = [remote(slab, slab, ws.at[3 + s], wr.at[3 + s], x_peers[s]) for s in range(3)]
    for c in cx:
        c.start()
    for c in cx:
        c.wait()
    slab = w_all.at[:, :, :, zc]
    cz = [remote(slab, slab, ws.at[6 + s], wr.at[6 + s], z_peers[s]) for s in range(3)]
    for c in cz:
        c.start()
    cc = [remote(slab, slab, ws.at[9], wr.at[9], c_peer)]
    cc[0].start()
    cu = [remote(u_ref, u_all.at[d], us.at[s], ur.at[s], depth_peers[s]) for s in range(7)]
    for c in cu:
        c.start()
    for s in range(3):
        cz[s].wait()
        there = w_all.at[:, :, :, ((z + 3 - s) % 4) * 2 + core]
        c = remote(there, there, ws.at[10 + s], wr.at[10 + s], c_peer)
        c.start()
        cc.append(c)
    for c in cc + cn + cu:
        c.wait()
    own[0].wait()
    own[1].wait()


def gather(normed, upstream, shard):
    any_spec = pl.BlockSpec(memory_space=pl.ANY)
    return pl.pallas_call(
        gather_kernel,
        out_shape=(
            jax.ShapeDtypeStruct((ND, ROWS, E), BF),
            jax.ShapeDtypeStruct((ND, ROWS, E), BF),
            jax.ShapeDtypeStruct((2, 4, 2, 8, 24, E), BF),
        ),
        in_specs=[any_spec] * 3,
        out_specs=(any_spec,) * 3,
        scratch_shapes=[
            pltpu.SemaphoreType.DMA((7,)),
            pltpu.SemaphoreType.DMA((7,)),
            pltpu.SemaphoreType.DMA((7,)),
            pltpu.SemaphoreType.DMA((7,)),
            pltpu.SemaphoreType.DMA((13,)),
            pltpu.SemaphoreType.DMA((13,)),
            pltpu.SemaphoreType.DMA((3,)),
        ],
        compiler_params=pltpu.CompilerParams(collective_id=1, has_side_effects=True),
        name="gather",
    )(normed, upstream, shard)


def attention_kernel(
    n_ref, u_ref, wq_ref, wk_ref, wv_ref, we_ref, p_ref, rs_ref,
    q_s, k_s, v_s, a_s, kt_s, vt_s, dk_s, dv_s, gq_s, go_s, gt_s,
):
    d, r, xh, y, xl, z, core = place()
    par = d % 2

    def project(c, _):
        rows = pl.ds(c * ROWS, ROWS)
        n = n_ref[c]
        q = (SCALE * dot(n, wq_ref[...], ((1,), (0,)))).astype(BF)
        k = dot(n, wk_ref[...], ((1,), (0,))).astype(BF)
        v = dot(n, wv_ref[...], ((1,), (0,))).astype(BF)
        a = dot(u_ref[c], we_ref[...], ((1,), (1,))).astype(BF)
        for h in range(2):
            cols = slice(h * HD, h * HD + HD)
            q_s[h, rows, :] = q[:, cols]
            k_s[h, rows, :] = k[:, cols]
            v_s[h, rows, :] = v[:, cols]
            a_s[h, rows, :] = a[:, cols]
        kt = k.T
        vt = v.T
        for h in range(2):
            rws = slice(h * HD, h * HD + HD)
            kt_s[h, c] = kt[rws]
            vt_s[h, c] = vt[rws]
        return 0

    lax.fori_loop(0, ND, project, 0)
    dk_s[...] = jnp.zeros_like(dk_s)
    dv_s[...] = jnp.zeros_like(dv_s)
    gq_s[...] = jnp.zeros_like(gq_s)
    go_s[...] = jnp.zeros_like(go_s)

    def step(i, _):
        h = i // 8
        c = jnp.where(h == 0, i, i - 8 + 4 * par)
        rows = pl.ds(pl.multiple_of(c * ROWS, ROWS), ROWS)
        q = q_s[h, rows, :]
        a = a_s[h, rows, :]
        st = dot(k_s[h], q, ((1,), (1,)))
        m = jnp.max(st, axis=0, keepdims=True)
        e = jnp.exp(st - m)
        p = e * (1.0 / jnp.sum(e, axis=0, keepdims=True))
        pb = p.astype(BF)
        dp = dot(v_s[h], a, ((1,), (1,)))
        delta = jnp.sum(p * dp, axis=0, keepdims=True)
        ds = (p * (dp - delta)).astype(BF)
        att = jnp.zeros((HD, ROWS), F32)
        dq = jnp.zeros((HD, ROWS), F32)
        for t in range(ND):
            ts = slice(t * ROWS, t * ROWS + ROWS)
            att += dot(vt_s[h, t], pb[ts], ((1,), (0,)))
            dq += dot(kt_s[h, t], ds[ts], ((1,), (0,)))
        att = att.astype(BF)
        dq = (SCALE * dq).astype(BF)
        dk_s[h] += dot(ds, q, ((1,), (0,)))
        dv_s[h] += dot(pb, a, ((1,), (0,)))
        go_s[h] += dot(att, u_ref[c], ((1,), (0,)))
        gq_s[h] += dot(dq, n_ref[c], ((1,), (0,)))
        base = pl.multiple_of(h * 384, 128)
        p_ref[c, pl.ds(base, HD), :] = att
        p_ref[c, pl.ds(base + HD, HD), :] = dq
        return 0

    lax.fori_loop(0, 12, step, 0)

    def finish(c, carry):
        rows = pl.ds(pl.multiple_of(c * ROWS, ROWS), ROWS)
        n = n_ref[c]
        out = []
        for h in range(2):
            dkt = dk_s[h, rows, :].T.astype(BF)
            dvt = dv_s[h, rows, :].T.astype(BF)
            p_ref[c, 128 + 128 * h:192 + 128 * h, :] = dkt
            p_ref[c, 192 + 128 * h:256 + 128 * h, :] = dvt
            gt_s[128 + h * HD:192 + h * HD] += dot(dkt, n, ((1,), (0,)))
            gt_s[256 + h * HD:320 + h * HD] += dot(dvt, n, ((1,), (0,)))
        return carry

    gt_s[...] = jnp.zeros_like(gt_s)
    lax.fori_loop(0, ND, finish, 0)
    gt_s[0:64] = gq_s[0]
    gt_s[64:128] = gq_s[1]
    gt = gt_s[...].astype(BF)
    go = jnp.concatenate([go_s[0], go_s[1]], axis=0).astype(BF)

    def order(b, _):
        R = lax.broadcasted_iota(jnp.int32, (256, E), 0) + b * 256
        F = lax.broadcasted_iota(jnp.int32, (256, E), 1)
        i = R % 8
        hit = (F == 6 * (16 * ((R // 8) % 8) + R // 64) + i) & (i < 6)
        hot = jnp.where(hit, 1.0, 0.0).astype(BF)
        g = dot(hot, gt, ((1,), (1,))).astype(BF)
        for s in range(4):
            rs_ref[4 * b + s, 0:64, :] = g[64 * s:64 * s + 64]
        return 0

    lax.fori_loop(0, 4, order, 0)
    R = lax.broadcasted_iota(jnp.int32, (256, 128), 0)
    C = lax.broadcasted_iota(jnp.int32, (256, 128), 1)
    i = R % 8
    feature = jnp.where(C < 64, C + 128 * par, C)
    hit = (feature == 96 * ((R // 8) % 2) + 6 * (R // 16) + i) & (i < 6)
    hot = jnp.where(hit, 1.0, 0.0).astype(BF)
    g = dot(hot, go, ((1,), (0,))).astype(BF)
    for s in range(NR):
        rs_ref[s, 64:80, :] = g[16 * s:16 * s + 16, 0:384]
        rs_ref[s, 80:96, :] = g[16 * s:16 * s + 16, 384:768]


def attention(n_all, u_all, wq, wk, wv, we):
    vm = pl.BlockSpec(memory_space=pltpu.VMEM)
    return pl.pallas_call(
        attention_kernel,
        out_shape=(
            jax.ShapeDtypeStruct((ND, 512, ROWS), BF),
            jax.ShapeDtypeStruct((NR, 96, 384), BF),
        ),
        in_specs=[vm] * 6,
        out_specs=(vm, vm),
        scratch_shapes=[pltpu.VMEM((2, SEQ, HD), BF)] * 4
        + [pltpu.VMEM((2, ND, HD, ROWS), BF)] * 2
        + [pltpu.VMEM((2, SEQ, HD), F32)] * 2
        + [pltpu.VMEM((2, HD, E), F32)] * 2
        + [pltpu.VMEM((384, E), F32)],
        compiler_params=pltpu.CompilerParams(vmem_limit_bytes=VMEM_LIMIT),
        name="attention",
    )(n_all, u_all, wq, wk, wv, we)


def exchange_kernel(
    p_ref, rs_ref, b_ref, fin_ref,
    bc, acc1, bz, acc2, bx, acc3, finq, fino, ps, pr, hs, hr, gs, gr, loc,
):
    d, r, xh, y, xl, z, core = place()
    par = d % 2
    zc = z * 2 + core
    depth_peers = [at((d + s) % ND, r) for s in range(1, ND)]
    z_peers = [at(d, xl * 8 + ((z + s) % 4) * 2 + core) for s in range(1, 4)]
    x_peer = at(d, (1 - xl) * 8 + zc)
    c_peer = at(d, xl * 8 + z * 2 + 1 - core)
    barrier(depth_peers + z_peers + [x_peer, c_peer])

    local = pltpu.make_async_copy(p_ref.at[d], b_ref.at[d], loc.at[0])
    local.start()
    cc = []
    for g in range(8):
        c = remote(rs_ref.at[2 * g + 1 - core], bc.at[g], gs.at[g], gr.at[g], c_peer)
        c.start()
        cc.append(c)
    cp = []
    for s in range(1, ND):
        to = (d + s) % ND
        c = remote(p_ref.at[to, 0:384], b_ref.at[d, 0:384], ps.at[s - 1], pr.at[s - 1], depth_peers[s - 1])
        c.start()
        cp.append(c)
    ch = []
    for s in range(1, ND):
        to = (d + s) % ND
        c = remote(p_ref.at[to, 384:512], b_ref.at[d, 384:512], hs.at[s - 1], hr.at[s - 1], depth_peers[s - 1])
        pl.when(to // 4 == par)(c.start)
        ch.append(c)
    for g in range(8):
        cc[g].wait()
        acc1[g] = (rs_ref[2 * g + core].astype(F32) + bc[g].astype(F32)).astype(BF)
    cz = []
    for s in range(1, 4):
        to = (z + s) % 4
        for x in range(2):
            k = (s - 1) * 2 + x
            c = remote(acc1.at[x * 4 + to], bz.at[s - 1, x], gs.at[8 + k], gr.at[8 + k], z_peers[s - 1])
            c.start()
            cz.append(c)
    for c in cz:
        c.wait()
    total = [
        acc1[x * 4 + z].astype(F32) + bz[0, x].astype(F32) + bz[1, x].astype(F32) + bz[2, x].astype(F32)
        for x in range(2)
    ]
    acc2[0] = total[0].astype(BF)
    acc2[1] = total[1].astype(BF)
    cx = remote(acc2.at[1 - xl], bx, gs.at[14], gr.at[14], x_peer)
    cx.start()
    cx.wait()
    acc3[...] = acc2[xl].astype(F32) + bx[...].astype(F32)
    last = []
    for s in range(1, ND):
        to = (d + s) % ND
        rows = pl.ds(pl.multiple_of(to * 8, 8), 8)
        c = remote(acc3.at[rows], finq.at[d], gs.at[14 + s], gr.at[14 + s], depth_peers[s - 1])
        c.start()
        last.append(c)
    partner = at(d + 1 - 2 * par, r)
    for half in range(2):
        rows = pl.ds(pl.multiple_of(64 + half * 16 + (1 - par) * 8, 8), 8)
        c = remote(acc3.at[rows], fino.at[half], gs.at[22 + half], gr.at[22 + half], partner)
        c.start()
        last.append(c)
    finq[d] = acc3[pl.ds(pl.multiple_of(d * 8, 8), 8), :]
    for c in last:
        c.wait()
    for j in range(4):
        for m in range(3):
            one = finq[2 * j, :, m * 128:m * 128 + 128]
            two = finq[2 * j + 1, :, m * 128:m * 128 + 128]
            fin_ref[m, :, 192 * j:192 * j + 192] = jnp.concatenate(
                [one[:, 0:64], one[:, 64:128] + two[:, 64:128], two[:, 0:64]], axis=1
            )
    for half in range(2):
        rows = pl.ds(pl.multiple_of(64 + half * 16 + par * 8, 8), 8)
        fin_ref[3, :, half * 384:half * 384 + 384] = acc3[rows, :] + fino[half]
    local.wait()
    for c in cp:
        c.wait()
    for s in range(1, ND):
        to = (d + s) % ND
        came = (d + ND - s) % ND
        pl.when(to // 4 == par)(ch[s - 1].wait_send)
        pl.when(came % 2 == d // 4)(ch[s - 1].wait_recv)


def exchange(p, rs):
    vm = pl.BlockSpec(memory_space=pltpu.VMEM)
    return pl.pallas_call(
        exchange_kernel,
        out_shape=(
            jax.ShapeDtypeStruct((ND, 512, ROWS), BF),
            jax.ShapeDtypeStruct((4, 8, E), F32),
        ),
        in_specs=[vm, vm],
        out_specs=(vm, vm),
        scratch_shapes=[
            pltpu.VMEM((8, 96, 384), BF),
            pltpu.VMEM((8, 96, 384), BF),
            pltpu.VMEM((3, 2, 96, 384), BF),
            pltpu.VMEM((2, 96, 384), BF),
            pltpu.VMEM((96, 384), BF),
            pltpu.VMEM((96, 384), F32),
            pltpu.VMEM((ND, 8, 384), F32),
            pltpu.VMEM((2, 8, 384), F32),
            pltpu.SemaphoreType.DMA((7,)),
            pltpu.SemaphoreType.DMA((7,)),
            pltpu.SemaphoreType.DMA((7,)),
            pltpu.SemaphoreType.DMA((7,)),
            pltpu.SemaphoreType.DMA((24,)),
            pltpu.SemaphoreType.DMA((24,)),
            pltpu.SemaphoreType.DMA((1,)),
        ],
        compiler_params=pltpu.CompilerParams(
            collective_id=2, has_side_effects=True, vmem_limit_bytes=VMEM_LIMIT
        ),
        name="exchange",
    )(p, rs)


def rows_kernel(b_ref, x_ref, u_ref, gain_ref, wq_ref, wk_ref, wv_ref, we_ref, out_ref, al_ref, t_s):
    half = lax.axis_index("depth") // 4
    for j in range(4):
        lo, hi = 2 * j, 2 * j + 1
        sh = 2 * j + half
        for m in range(4):
            t_s[m, 192 * j:192 * j + 64] = b_ref[lo, 64 * m:64 * m + 64]
            t_s[m, 192 * j + 128:192 * j + 192] = b_ref[hi, 64 * m:64 * m + 64]
        for m in range(2):
            t_s[m, 192 * j + 64:192 * j + 128] = b_ref[sh, 384 + 64 * m:448 + 64 * m]
            rows = slice(256 + 64 * m, 320 + 64 * m)
            t_s[2 + m, 192 * j + 64:192 * j + 128] = (
                b_ref[lo, rows].astype(F32) + b_ref[hi, rows].astype(F32)
            ).astype(BF)
    x = x_ref[...].astype(F32)
    att = t_s[0].T
    out_ref[...] = (x + dot(att, we_ref[...], ((1,), (0,)))).astype(BF)
    dn = dot(t_s[1].T, wq_ref[...], ((1,), (1,)))
    dn += dot(t_s[2].T, wk_ref[...], ((1,), (1,)))
    dn += dot(t_s[3].T, wv_ref[...], ((1,), (1,)))
    centered = x - jnp.mean(x, axis=-1, keepdims=True)
    inverse = lax.rsqrt(jnp.mean(centered * centered, axis=-1, keepdims=True) + 1e-05)
    unit = centered * inverse
    du = dn * gain_ref[...]
    al_ref[...] = (
        u_ref[...].astype(F32)
        + inverse
        * (du - jnp.mean(du, axis=-1, keepdims=True) - unit * jnp.mean(du * unit, axis=-1, keepdims=True))
    ).astype(BF)


def rows_results(back, x, u, gain, wq, wk, wv, we):
    vm = pl.BlockSpec(memory_space=pltpu.VMEM)
    return pl.pallas_call(
        rows_kernel,
        out_shape=(jax.ShapeDtypeStruct((ROWS, E), BF), jax.ShapeDtypeStruct((ROWS, E), BF)),
        in_specs=[vm] * 8,
        out_specs=(vm, vm),
        scratch_shapes=[pltpu.VMEM((4, E, ROWS), BF)],
        compiler_params=pltpu.CompilerParams(vmem_limit_bytes=VMEM_LIMIT),
        name="rows",
    )(back, x, u, gain, wq, wk, wv, we)


def body(x, gain, wq, wk, wv, we, u):
    x = x.reshape(ROWS, E)
    u = u.reshape(ROWS, E)
    xf = x.astype(F32)
    centered = xf - jnp.mean(xf, axis=-1, keepdims=True)
    inverse = lax.rsqrt(jnp.mean(centered * centered, axis=-1, keepdims=True) + 1e-05)
    normed = (centered * inverse * gain).astype(BF)
    shard = jnp.concatenate([wq, wk, wv, we], axis=0)
    n_all, u_all, w_all = gather(normed, u, shard)
    w_full = w_all.reshape(128, 4, 6, E).transpose(1, 0, 2, 3).reshape(4, E, E)
    d = lax.axis_index("depth")
    r = lax.axis_index("res")
    j, par = d // 2, d % 2

    def columns(w):
        three = lax.dynamic_slice(w, (0, 192 * j), (E, 192))
        return jnp.concatenate(
            [jnp.where(par == 0, three[:, 0:64], three[:, 128:192]), three[:, 64:128]], axis=1
        )

    three = lax.dynamic_slice(w_full[3], (192 * j, 0), (192, E))
    we_own = jnp.concatenate([jnp.where(par == 0, three[0:64], three[128:192]), three[64:128]], axis=0)
    p, rs = attention(n_all, u_all, columns(w_full[0]), columns(w_full[1]), columns(w_full[2]), we_own)
    back, fin = exchange(p, rs)
    out, al = rows_results(
        back, x, u, gain.reshape(1, E), w_full[0], w_full[1], w_full[2], w_full[3]
    )
    gq, gk, gv, go = fin[0, :6], fin[1, :6], fin[2, :6], fin[3, :6]
    own_gain = lax.dynamic_slice(gain, (6 * (NR * d + r),), (6,))
    dgain = (
        jnp.sum(gq * wq.astype(F32) + gk * wk.astype(F32) + gv * wv.astype(F32), axis=1) / own_gain
    )
    return out.reshape(ROWS, 1, E), al.reshape(ROWS, 1, E), gq, gk, gv, go, dgain


def solution(mesh):
    rows = P("depth", "res", None)
    shard = P(("depth", "res"), None)
    return jax.shard_map(
        body,
        mesh=mesh,
        in_specs=(rows, P(), shard, shard, shard, shard, rows),
        out_specs=(rows, rows, shard, shard, shard, shard, P(("depth", "res"))),
        check_vma=False,
    )
```

time: 2020 us -> 227 us (0.11)
  waiting for transfers between devices: 979 us -> 0 us
  blocking collectives: 428 us -> 0 us
  starting transfers between devices: 354 us -> 0 us
  Pallas kernels: 0 us -> 198 us
  matrix products: 136 us -> 0 us
  local copies, waits for them, and re-layouts: 71.3 us -> 18 us
    all_gather x6 -> x0, waiting for transfers between devices: 882 us -> none  [the longest x1 193 us: body(): lax.all_gather(lookup_weights, ('depth', 'res'), axis=0, tiled=True)]
    unnamed x2 -> x0, blocking collectives: 428 us -> none
    unnamed x128 -> x0, starting transfers between devices: 354 us -> none
    pallas_call x0 -> x4, Pallas kernels: none -> 198 us  [the longest x1 97 us: gather(): pl.pallas_call(gather_kernel, out_shape=(jax.ShapeDtypeStruct((ND, ROWS,...]
    dot_general x84 -> x0, matrix products: 136 us -> none  [the longest x12 25.7 us: head_pass(): jnp.dot(probs_b, payload_entries, preferred_element_type=jnp.float32)]
    reduce_scatter x1 -> x0, waiting for transfers between devices: 91.9 us -> none  [body(): lax.psum_scatter(stacked, 'depth', scatter_dimension=0, tiled=True)]
    unnamed x239 -> x30, local copies, waits for them, and re-layouts: 61.6 us -> 0.74 us
  transfers between devices with their start and end apart: 135 -> 0, of which waited for: 9 -> 0; matrix products, arithmetic and copies ran while one was open for 4% -> 0% of each run, Pallas kernels for 0% -> 0%
where the time goes in v1:
time: 227 us
  Pallas kernels  198 us (87%)
  local copies, waits for them, and re-layouts  18 us (8%)
  other arithmetic  10.2 us (4%)
    pallas_call x1, Pallas kernels, gather(): pl.pallas_call(gather_kernel, out_shape=(jax.ShapeDtypeStruct((ND, ROWS,...  97 us
    pallas_call x1, Pallas kernels, attention(): pl.pallas_call(attention_kernel, out_shape=(jax.ShapeDtypeStruct((ND, 512...  49 us
    pallas_call x1, Pallas kernels, exchange(): pl.pallas_call(exchange_kernel, out_shape=(jax.ShapeDtypeStruct((ND, 512,...  46.1 us
    pallas_call x1, Pallas kernels, rows_results(): pl.pallas_call(rows_kernel, out_shape=(jax.ShapeDtypeStruct((ROWS, E), BF...  5.65 us

profile of v1, /device:TPU:0, one launch (start us, length us, event | category | flops | bytes accessed | tf_op | source)
XLA Modules:
  0.0 227.0 jit_solution(17454042792887985883)
XLA Ops:
  0.6 0.0 copy-start.14
  0.6 0.0 copy-start.8
  0.7 0.0 copy-start.9
  0.7 0.0 copy-start.11
  0.7 1.1 convert_reduce_fusion
  1.8 1.2 fusion.2
  3.1 2.0 fusion.4.n_ref
  5.1 0.0 copy-done.14
  5.1 0.0 copy-done.8
  5.1 0.0 copy-done.9
  5.1 0.0 copy-done.11
  5.1 0.6 pad_maximum_fusion.4.w_ref
  5.7 97.0 %gather.1 = (bf16[8,256,768]{2,1,0:T(8,128)(2,1)}, bf16[8,256,768]{2,1,0:T(8,128)(2,1)}, bf16[2,4,2,8,24,768]{5,4,3,2,1,0:T(8,128)(2,1)}) custom-call(bf16[256,768]{1,0:T(8,128)(2,1)} %fusion.4.n_ref, bf16[256,768]{1,0:T(8,128)(2,1)} %bitcast.23, bf16[24,768]{1,0:T(8,128)(2,1)} %pad_maximum_fusion.4.w_ref), custom_call_target="tpu_custom_call" | custom-call | tf_op jit(solution)/shard_map/gather/pallas_call | solution.py:104
  102.8 3.4 %copy.15 = bf16[2,4,2,8,24,768]{5,3,2,1,0,4:T(8,128)(2,1)S(1)} copy(bf16[2,4,2,8,24,768]{5,4,3,2,1,0:T(8,128)(2,1)} %get-tuple-element.18) | data formatting | bytes 9437184 | tf_op jit(solution)/shard_map/gather/pallas_call | solution.py:104
  106.2 1.9 fusion.5
  108.1 0.7 copy.16
  108.8 0.6 squeeze.28.wq_ref
  109.4 0.0 copy-start.2
  109.4 0.0 copy-start.6
  109.4 0.2 dynamic-slice_select_fusion.2
  109.7 0.8 pad_maximum_fusion.wq_ref
  110.5 0.7 copy-done.6
  111.2 1.8 copy.18
  113.0 0.0 copy-done.2
  113.0 2.4 %squeeze.30.wv_ref = bf16[768,768]{1,0:T(8,128)(2,1)S(1)} reshape(bf16[1,128,6,768]{3,2,1,0:T(8,128)(2,1)} %copy.18) | data formatting | bytes 2359296 | tf_op jit(solution)/shard_map/squeeze | solution.py:449
  115.4 0.0 copy-start
  115.4 0.0 copy-done.5
  115.4 1.8 copy.17
  117.3 2.3 %squeeze.29.wk_ref = bf16[768,768]{1,0:T(8,128)(2,1)S(1)} reshape(bf16[1,128,6,768]{3,2,1,0:T(8,128)(2,1)} %copy.17) | data formatting | bytes 2359296 | tf_op jit(solution)/shard_map/squeeze | solution.py:449
  119.6 0.0 copy-done
  119.6 0.0 copy-start.1
  119.6 0.0 copy-start.4
  119.6 0.4 dynamic-slice_select_fusion
  120.0 0.8 pad_maximum_fusion.1.wk_ref
  120.8 0.0 copy-done.1
  120.8 0.8 pad_maximum_fusion.2.wv_ref
  121.6 0.0 copy-done.4
  121.6 0.7 copy.19
  122.3 0.4 squeeze.31.we_ref
  122.8 0.8 pad_maximum_fusion.3.we_ref
  123.6 49.0 %attention.1 = (bf16[8,512,256]{2,1,0:T(8,128)(2,1)}, bf16[16,96,384]{2,1,0:T(8,128)(2,1)}) custom-call(bf16[8,256,768]{2,1,0:T(8,128)(2,1)} %get-tuple-element.16.n_ref, bf16[8,256,768]{2,1,0:T(8,128)(2,1)} %get-tuple-element.17.u_ref, bf16[768,128]{1,0:T(8,128)(2,1)} %pad_maximum_fusion.wq_ref, bf16[768,128]{1,0:T(8,128)(2,1)} %pad_maximum_fusion.1.wk_ref, ...), custom_call_target="tpu_custom_call" | custom-call | tf_op jit(solution)/shard_map/attention/pallas_call | solution.py:240
  172.6 46.1 %exchange.1 = (bf16[8,512,256]{2,1,0:T(8,128)(2,1)}, f32[4,8,768]{2,1,0:T(8,128)}) custom-call(bf16[8,512,256]{2,1,0:T(8,128)(2,1)} %get-tuple-element.19.p_ref, bf16[16,96,384]{2,1,0:T(8,128)(2,1)} %get-tuple-element.20.rs_ref), custom_call_target="tpu_custom_call" | custom-call | tf_op jit(solution)/shard_map/exchange/pallas_call | solution.py:351
  218.8 0.6 broadcast_in_dim.2.gain_ref
  219.3 5.7 %rows.1 = (bf16[256,768]{1,0:T(8,128)(2,1)}, bf16[256,768]{1,0:T(8,128)(2,1)}) custom-call(bf16[8,512,256]{2,1,0:T(8,128)(2,1)} %get-tuple-element.21.b_ref, bf16[256,768]{1,0:T(8,128)(2,1)} %bitcast.22, bf16[256,768]{1,0:T(8,128)(2,1)} %bitcast.24, f32[1,768]{1,0:T(1,128)} %broadcast_in_dim.2.gain_ref, bf16[768,768]{1,0:T(8,128)(2,1)} %copy-done.2, ...), custom_call_target="tpu_custom_call" | custom-call | tf_op jit(solution)/shard_map/rows/pallas_call | solution.py:416
  225.0 0.0 copy-done.10
  225.0 0.7 add_reduce_fusion
  225.8 0.6 slice_bitcast_fusion
  226.4 0.6 dynamic-slice_divide_fusion
  (13 shorter events, 0.1 us)
Async XLA Ops:
  0.6 4.4 %copy-start.14 = (bf16[6,768]{1,0:T(8,128)(2,1)S(1)}, bf16[6,768]{1,0:T(8,128)(2,1)}, u32[]{:S(2)}) copy-start(bf16[6,768]{1,0:T(8,128)(2,1)} %param.12) | copy-start | bytes 27652
  0.6 4.4 %copy-start.8 = (bf16[6,768]{1,0:T(8,128)(2,1)S(1)}, bf16[6,768]{1,0:T(8,128)(2,1)}, u32[]{:S(2)}) copy-start(bf16[6,768]{1,0:T(8,128)(2,1)} %param.11) | copy-start | bytes 27652
  0.7 4.4 %copy-start.9 = (bf16[6,768]{1,0:T(8,128)(2,1)S(1)}, bf16[6,768]{1,0:T(8,128)(2,1)}, u32[]{:S(2)}) copy-start(bf16[6,768]{1,0:T(8,128)(2,1)} %param.10) | copy-start | bytes 27652
  0.7 4.4 %copy-start.11 = (bf16[6,768]{1,0:T(8,128)(2,1)S(1)}, bf16[6,768]{1,0:T(8,128)(2,1)}, u32[]{:S(2)}) copy-start(bf16[6,768]{1,0:T(8,128)(2,1)} %param.9) | copy-start | bytes 27652
  109.4 3.6 %copy-start.2 = (bf16[768,768]{1,0:T(8,128)(2,1)}, bf16[768,768]{1,0:T(8,128)(2,1)S(1)}, u32[]{:S(2)}) copy-start(bf16[768,768]{1,0:T(8,128)(2,1)S(1)} %squeeze.28.wq_ref) | copy-start | bytes 3538948
  109.4 1.8 copy-start.6
  113.0 2.4 %copy-start.5 = (bf16[1,128,6,768]{3,1,2,0:T(8,128)(2,1)S(1)}, bf16[1,128,6,768]{3,1,2,0:T(8,128)(2,1)}, u32[]{:S(2)}) copy-start(bf16[1,128,6,768]{3,1,2,0:T(8,128)(2,1)} %get-tuple-element.31) | copy-start | bytes 3538948
  115.4 4.2 %copy-start = (bf16[768,768]{1,0:T(8,128)(2,1)}, bf16[768,768]{1,0:T(8,128)(2,1)S(1)}, u32[]{:S(2)}) copy-start(bf16[768,768]{1,0:T(8,128)(2,1)S(1)} %squeeze.30.wv_ref) | copy-start | bytes 3538948
  119.6 1.2 copy-start.1
  119.6 2.0 copy-start.4
  122.7 49.9 %copy-start.3 = (bf16[768,768]{1,0:T(8,128)(2,1)}, bf16[768,768]{1,0:T(8,128)(2,1)S(1)}, u32[]{:S(2)}) copy-start(bf16[768,768]{1,0:T(8,128)(2,1)S(1)} %squeeze.31.we_ref) | copy-start | bytes 3538948
  172.6 46.1 %copy-start.13 = (f32[768]{0:T(1024)S(1)}, f32[768]{0:T(1024)}, u32[]{:S(2)}) copy-start(f32[768]{0:T(1024)} %param.8) | copy-start | bytes 9220
  219.3 5.7 %copy-start.7 = (f32[4,8,768]{2,1,0:T(8,128)S(1)}, f32[4,8,768]{2,1,0:T(8,128)}, u32[]{:S(2)}) copy-start(f32[4,8,768]{2,1,0:T(8,128)} %get-tuple-element.24) | copy-start | bytes 294916
  219.3 5.7 %copy-start.10 = (bf16[6,768]{1,0:T(8,128)(2,1)S(1)}, bf16[6,768]{1,0:T(8,128)(2,1)}, u32[]{:S(2)}) copy-start(bf16[6,768]{1,0:T(8,128)(2,1)} %param.10) | copy-start | bytes 27652
  219.3 5.7 %copy-start.12 = (bf16[6,768]{1,0:T(8,128)(2,1)S(1)}, bf16[6,768]{1,0:T(8,128)(2,1)}, u32[]{:S(2)}) copy-start(bf16[6,768]{1,0:T(8,128)(2,1)} %param.9) | copy-start | bytes 27652

commit v2 on v0

v2 whole, which is shorter than its diff:
```python
import jax
import jax.numpy as jnp
from jax import lax
from jax.experimental import pallas as pl
from jax.experimental.pallas import tpu as pltpu
from jax.sharding import PartitionSpec as P

HD = 64
E = 768
ND = 8
NR = 16
ROWS = 256
SEQ = ND * ROWS
TILE = 256
SCALE = HD ** (-0.5)
MESH = pl.DeviceIdType.MESH
BF = jnp.bfloat16
F32 = jnp.float32
VMEM_LIMIT = 58 * 1024 * 1024


def place():
    d = lax.axis_index("depth")
    r = lax.axis_index("res")
    return d, r, d // 4, d % 4, r // 8, (r // 2) % 4, r % 2


def at(d, r):
    return {"depth": d, "res": r}


def barrier(peers):
    sem = pltpu.get_barrier_semaphore()
    for peer in peers:
        pl.semaphore_signal(sem, inc=1, device_id=peer, device_id_type=MESH)
    pl.semaphore_wait(sem, len(peers))


def remote(src, dst, send, recv, peer):
    return pltpu.make_async_remote_copy(
        src_ref=src, dst_ref=dst, send_sem=send, recv_sem=recv, device_id=peer, device_id_type=MESH
    )


def start(copies):
    for c in copies:
        c.start()


def wait(copies):
    for c in copies:
        c.wait()


def dot(a, b, ca, cb):
    return lax.dot_general(a, b, (((ca,), (cb,)), ((), ())), preferred_element_type=F32)


def hot(mask):
    return jnp.where(mask, 1.0, 0.0).astype(BF)


def moved(a, b, ca, cb):
    return dot(a, b, ca, cb).astype(BF)


def ring(src, full, d, xh, y, r, ss, rs):
    e = (d + 4) % ND
    up, down = at(xh * 4 + (y + 1) % 4, r), at(xh * 4 + (y + 3) % 4, r)
    lo, hi = xh * 4 + (y + 3) % 4, xh * 4 + (y + 1) % 4
    lo2, hi2 = (lo + 4) % ND, (hi + 4) % ND

    def near(k, peer, block, k0):
        return remote(block, k, ss.at[k0], rs.at[k0], peer)

    c0 = near(full.at[d], at(e, r), src, 0)
    a = near(full.at[d], up, src, 1)
    b = near(full.at[d], down, src, 2)
    a2 = near(full.at[e], up, full.at[e], 3)
    b2 = near(full.at[e], down, full.at[e], 4)
    f1 = near(full.at[lo, 0:128], up, full.at[lo, 0:128], 5)
    f2 = near(full.at[hi, 128:256], down, full.at[hi, 128:256], 6)
    g1 = near(full.at[lo2, 0:128], up, full.at[lo2, 0:128], 7)
    g2 = near(full.at[hi2, 128:256], down, full.at[hi2, 128:256], 8)
    return c0, (a, b), (a2, b2), (f1, f2), (g1, g2)


def kernel(
    x_ref, u_ref, gain_ref, wq_ref, wk_ref, wv_ref, we_ref,
    out_ref, al_ref, gq_ref, gk_ref, gv_ref, go_ref, dg_ref,
    n_all, u_all, wl, wr, wc, w_full, hot_s, sel_s,
    q_s, k_s, v_s, a_s, kt_s, vt_s, a_out, a_in, lse_s, p_s, dp_s, dk_s, dv_s,
    p_buf, b_buf, gt_s, ga_s, rs, bc, acc1, bz, acc2, bx, acc3, finq, fino, t_s,
    ns, nr, us, ur, ws, wrs, as_, ar, ps, pr, gs, gr, loc,
):
    d, r, xh, y, xl, z, core = place()
    par, j, half = d % 2, d // 2, d // 4
    zc = z * 2 + core
    depth_peers = [at((d + s) % ND, r) for s in range(1, ND)]
    y_peers = [at(xh * 4 + (y + s) % 4, r) for s in range(1, 4)]
    x_peers = [at((1 - xh) * 4 + y, r), at(d, (1 - xl) * 8 + zc), at((1 - xh) * 4 + y, (1 - xl) * 8 + zc)]
    z_peers = [at(d, xl * 8 + ((z + s) % 4) * 2 + core) for s in range(1, 4)]
    z_from = [((z + 4 - s) % 4) * 2 + core for s in range(1, 4)]
    c_peer = at(d, xl * 8 + z * 2 + 1 - core)
    barrier(depth_peers + x_peers[1:] + z_peers + [c_peer])

    top = jnp.concatenate(
        [wq_ref[...].astype(F32), wk_ref[...].astype(F32), wv_ref[0:4].astype(F32)], axis=0
    )
    rest = jnp.concatenate([wv_ref[4:6].astype(F32), we_ref[...].astype(F32)], axis=0)
    rest = jnp.concatenate([rest[:, 0:384], rest[:, 384:768]], axis=0)
    wl[xh, y, xl, zc] = top.astype(BF)
    wr[xh, y, xl, zc] = rest.astype(BF)
    wy = []
    for s in range(3):
        for k, w in enumerate((wl, wr)):
            one = w.at[xh, y, xl, zc]
            wy.append(remote(one, one, ws.at[2 * s + k], wrs.at[2 * s + k], y_peers[s]))
    start(wy)

    x = x_ref[...].astype(F32)
    centered = x - jnp.mean(x, axis=-1, keepdims=True)
    inverse = lax.rsqrt(jnp.mean(centered * centered, axis=-1, keepdims=True) + 1e-05)
    n_all[d] = (centered * inverse * gain_ref[...]).astype(BF)
    n0, n1, n2, n3, n4 = ring(n_all.at[d], n_all, d, xh, y, r, ns, nr)
    n0.start()
    start(n1)
    own_u = pltpu.make_async_copy(u_ref, u_all.at[d], loc.at[0])
    own_u.start()

    window = pl.multiple_of(128 * ((3 * j) // 2), 128)
    offset = 192 * j - 128 * ((3 * j) // 2)
    R = lax.broadcasted_iota(jnp.int32, (96, 256), 0)
    K = lax.broadcasted_iota(jnp.int32, (96, 256), 1)
    o16, i6 = 16 * (R // 6), R % 6
    hot_s[0] = hot(K == o16 + i6)
    hot_s[1] = hot(K == o16 + 6 + i6)
    hot_s[2] = hot((K == o16 + 12 + i6) & (i6 < 4))
    hot_s[3] = hot((K == o16 + i6 - 4) & (i6 >= 4))
    hot_s[4] = hot((K == o16 + 8 + i6 - 4) & (i6 >= 4))
    hot_s[5] = hot(K == o16 + 2 + i6)
    hot_s[6] = hot(K == o16 + 10 + i6)
    K2 = lax.broadcasted_iota(jnp.int32, (256, 128), 0)
    C2 = lax.broadcasted_iota(jnp.int32, (256, 128), 1)
    pick = hot(K2 == jnp.where(C2 < 64, offset + 128 * par + C2, offset + C2))
    p_buf[:, 384:512, :] = jnp.zeros((ND, 128, ROWS), BF)

    wait(wy)
    wx = []
    for s in range(3):
        for k, w in enumerate((wl, wr)):
            slab = w.at[xh, :, xl, zc]
            wx.append(remote(slab, slab, ws.at[6 + 2 * s + k], wrs.at[6 + 2 * s + k], x_peers[s]))
    start(wx)
    n0.wait()
    start(n2)
    wait(n1)
    start(n3)
    wait(wx)

    mine = wl.at[:, :, :, zc, :, pl.ds(window, 256)]
    wz1 = [remote(mine, wc.at[:, :, :, zc], ws.at[12 + s], wrs.at[12 + s], z_peers[s]) for s in range(3)]
    start(wz1)
    wc1 = [remote(mine, wc.at[:, :, :, zc], ws.at[15], wrs.at[15], c_peer)]
    start(wc1)
    own_w = pltpu.make_async_copy(mine, wc.at[:, :, :, zc], loc.at[1])
    own_w.start()
    slab = wr.at[:, :, :, zc]
    wz2 = [remote(slab, slab, ws.at[19 + s], wrs.at[19 + s], z_peers[s]) for s in range(3)]
    start(wz2)
    wc2 = [remote(slab, slab, ws.at[22], wrs.at[22], c_peer)]
    start(wc2)
    for s in range(3):
        wz1[s].wait()
        there = wc.at[:, :, :, z_from[s]]
        c = remote(there, there, ws.at[16 + s], wrs.at[16 + s], c_peer)
        c.start()
        wc1.append(c)
    wait(n2)
    start(n4)
    slab = wl.at[:, :, :, zc]
    wz3 = [remote(slab, slab, ws.at[26 + s], wrs.at[26 + s], z_peers[s]) for s in range(3)]
    start(wz3)
    wc3 = [remote(slab, slab, ws.at[29], wrs.at[29], c_peer)]
    start(wc3)
    wait(wc1)
    own_w.wait()

    for g in range(8):
        s1 = moved(wc[g // 4, g % 4].reshape(256, 256), pick, 1, 0)
        rows = slice(96 * g, 96 * g + 96)
        sel_s[0, rows] = moved(hot_s[0], s1, 1, 0)
        sel_s[1, rows] = moved(hot_s[1], s1, 1, 0)
        sel_s[2, rows] = moved(hot_s[2], s1, 1, 0)
    wait(n3)
    wait(n4)

    def project_qk(c, _):
        rows = pl.ds(pl.multiple_of(c * ROWS, ROWS), ROWS)
        n = n_all[c]
        q = (SCALE * dot(n, sel_s[0], 1, 0)).astype(BF)
        k = dot(n, sel_s[1], 1, 0).astype(BF)
        kt = k.T
        for h in range(2):
            q_s[h, rows, :] = q[:, h * HD:h * HD + HD]
            k_s[h, rows, :] = k[:, h * HD:h * HD + HD]
            kt_s[h, c] = kt[h * HD:h * HD + HD]
        return 0

    lax.fori_loop(0, ND, project_qk, 0)

    def stats(h, c):
        q = q_s[h, pl.ds(pl.multiple_of(c * ROWS, ROWS), ROWS), :]
        m = jnp.full((8, ROWS), -jnp.inf, F32)
        l = jnp.zeros((8, ROWS), F32)
        for t in range(SEQ // TILE):
            s = dot(k_s[h, t * TILE:t * TILE + TILE, :], q, 1, 1).reshape(TILE // 8, 8, ROWS)
            new = jnp.maximum(m, jnp.max(s, axis=0))
            l = l * jnp.exp(m - new) + jnp.sum(jnp.exp(s - new[None]), axis=0)
            m = new
        top = jnp.max(m, axis=0, keepdims=True)
        lse_s[h, c] = top + jnp.log(jnp.sum(l * jnp.exp(m - top), axis=0, keepdims=True))

    def stats_shared(i, _):
        stats(1, 4 * par + i)
        return 0

    def stats_own(i, _):
        stats(0, i)
        return 0

    for s in range(3):
        wz2[s].wait()
        there = wr.at[:, :, :, z_from[s]]
        c = remote(there, there, ws.at[23 + s], wrs.at[23 + s], c_peer)
        c.start()
        wc2.append(c)
    lax.fori_loop(0, 4, stats_shared, 0)
    wait(wc2)

    for g in range(8):
        s2 = wr[g // 4, g % 4].reshape(256, 384)
        rows = slice(96 * g, 96 * g + 96)
        w_full[3, rows, 0:384] = moved(hot_s[5], s2, 1, 0)
        w_full[3, rows, 384:768] = moved(hot_s[6], s2, 1, 0)
    a = dot(u_ref[...], w_full[3], 1, 1).astype(BF)
    for t in range(ND):
        own, sh = 192 * (t // 2) + 128 * (t % 2), 192 * (t // 2) + 64
        a_out[t] = jnp.concatenate([a[:, own:own + HD], a[:, sh:sh + HD]], axis=1)
    ca = []
    for s in range(1, ND):
        c = remote(a_out.at[(d + s) % ND], a_in.at[d], as_.at[s - 1], ar.at[s - 1], depth_peers[s - 1])
        c.start()
        ca.append(c)
    u0, u1, u2, u3, u4 = ring(u_ref, u_all, d, xh, y, r, us, ur)
    u0.start()
    start(u1)
    a_in[d] = a_out[d]

    inner = pl.multiple_of(128 * ((3 * j) // 2) - 384 * half, 128)
    for g in range(8):
        s2 = moved(wr[g // 4, g % 4, :, :, :, pl.ds(inner, 256)].reshape(256, 256), pick, 1, 0)
        late = jnp.where(half == 0, hot_s[3], hot_s[4])
        rows = slice(96 * g, 96 * g + 96)
        sel_s[2, rows] = sel_s[2, rows] + moved(late, s2, 1, 0)

    def project_v(c, _):
        rows = pl.ds(pl.multiple_of(c * ROWS, ROWS), ROWS)
        v = dot(n_all[c], sel_s[2], 1, 0).astype(BF)
        vt = v.T
        for h in range(2):
            v_s[h, rows, :] = v[:, h * HD:h * HD + HD]
            vt_s[h, c] = vt[h * HD:h * HD + HD]
        return 0

    lax.fori_loop(0, ND, project_v, 0)
    lax.fori_loop(0, 8, stats_own, 0)
    wait(ca)

    def spread(c, _):
        rows = pl.ds(pl.multiple_of(c * ROWS, ROWS), ROWS)
        got = a_in[c]
        a_s[0, rows, :] = got[:, 0:HD]
        a_s[1, rows, :] = got[:, HD:2 * HD]
        return 0

    lax.fori_loop(0, ND, spread, 0)
    u0.wait()
    start(u2)
    wait(u1)
    start(u3)
    for s in range(3):
        wz3[s].wait()
        there = wl.at[:, :, :, z_from[s]]
        c = remote(there, there, ws.at[30 + s], wrs.at[30 + s], c_peer)
        c.start()
        wc3.append(c)

    def attend(h, c, base):
        rows = pl.ds(pl.multiple_of(c * ROWS, ROWS), ROWS)
        q = q_s[h, rows, :]
        a = a_s[h, rows, :]
        qt, at_ = q.T, a.T
        lse = lse_s[h, c]
        delta = jnp.zeros((8, ROWS), F32)
        for t in range(SEQ // TILE):
            ts = slice(t * TILE, t * TILE + TILE)
            p = jnp.exp(dot(k_s[h, ts, :], q, 1, 1) - lse)
            dp = dot(v_s[h, ts, :], a, 1, 1)
            p_s[ts, :] = p
            dp_s[ts, :] = dp
            delta = delta + jnp.sum((p * dp).reshape(TILE // 8, 8, ROWS), axis=0)
        delta = jnp.sum(delta, axis=0, keepdims=True)
        att = jnp.zeros((HD, ROWS), F32)
        dq = jnp.zeros((HD, ROWS), F32)
        for t in range(SEQ // TILE):
            ts = slice(t * TILE, t * TILE + TILE)
            p = p_s[ts, :]
            pb = p.astype(BF)
            ds = (p * (dp_s[ts, :] - delta)).astype(BF)
            att += dot(vt_s[h, t], pb, 1, 0)
            dq += dot(kt_s[h, t], ds, 1, 0)
            dk_s[:, ts] += dot(qt, ds, 1, 1)
            dv_s[:, ts] += dot(at_, pb, 1, 1)
        p_buf[c, base:base + HD, :] = att.astype(BF)
        p_buf[c, base + HD:base + 2 * HD, :] = (SCALE * dq).astype(BF)

    def sent(kind, c):
        rows = slice((0, 128, 256, 384)[kind], (128, 256, 384, 512)[kind])
        return remote(
            p_buf.at[c, rows], b_buf.at[d, rows], ps.at[kind, c], pr.at[kind, d], at(c, r)
        )

    def came(kind, c):
        rows = slice((0, 128, 256, 384)[kind], (128, 256, 384, 512)[kind])
        return remote(
            p_buf.at[c, rows], b_buf.at[c, rows], ps.at[kind, c], pr.at[kind, c], at(c, r)
        )

    def totals(base, kind):
        for c in range(ND):
            cols = slice(c * ROWS, c * ROWS + ROWS)
            p_buf[c, base:base + HD, :] = dk_s[:, cols].astype(BF)
            p_buf[c, base + HD:base + 2 * HD, :] = dv_s[:, cols].astype(BF)
        for s in range(1, ND):
            sent(kind, (d + s) % ND).start()

    def attend_shared(i, _):
        c = 4 * par + i
        attend(1, c, 384)
        pl.when(c != d)(lambda: sent(3, c).start())
        return 0

    def attend_own(c, _):
        attend(0, c, 0)
        pl.when(c != d)(lambda: sent(0, c).start())
        return 0

    dk_s[...] = jnp.zeros_like(dk_s)
    dv_s[...] = jnp.zeros_like(dv_s)
    lax.fori_loop(0, 4, attend_shared, 0)
    totals(256, 2)
    wait(u2)
    start(u4)
    dk_s[...] = jnp.zeros_like(dk_s)
    dv_s[...] = jnp.zeros_like(dv_s)
    lax.fori_loop(0, 8, attend_own, 0)
    totals(128, 1)
    local = pltpu.make_async_copy(p_buf.at[d], b_buf.at[d], loc.at[2])
    local.start()
    wait(u3)
    wait(u4)
    own_u.wait()

    gt_s[...] = jnp.zeros_like(gt_s)
    ga_s[...] = jnp.zeros_like(ga_s)

    def grads(c, _):
        n, u = n_all[c], u_all[c]
        gt_s[0:320] += dot(p_buf[c, 64:384], n, 1, 0)
        gt_s[320:384] += dot(p_buf[c, 448:512], n, 1, 0)
        ga_s[0:64] += dot(p_buf[c, 0:64], u, 1, 0)
        ga_s[64:128] += dot(p_buf[c, 384:448], u, 1, 0)
        return 0

    lax.fori_loop(0, ND, grads, 0)
    gt = gt_s[...].astype(BF)
    ga = ga_s[...].astype(BF)

    def order(b, _):
        R = lax.broadcasted_iota(jnp.int32, (256, E), 0) + b * 256
        F = lax.broadcasted_iota(jnp.int32, (256, E), 1)
        i = R % 8
        g = moved(hot((F == 6 * (16 * ((R // 8) % 8) + R // 64) + i) & (i < 6)), gt, 1, 1)
        for s in range(4):
            rs[4 * b + s, 0:64, :] = g[64 * s:64 * s + 64]
        return 0

    lax.fori_loop(0, 4, order, 0)
    R = lax.broadcasted_iota(jnp.int32, (256, 128), 0)
    C = lax.broadcasted_iota(jnp.int32, (256, 128), 1)
    i = R % 8
    feature = jnp.where(C < 64, C + 128 * par, C)
    g = moved(hot((feature == 96 * ((R // 8) % 2) + 6 * (R // 16) + i) & (i < 6)), ga, 1, 0)
    for s in range(NR):
        rs[s, 64:80, :] = g[16 * s:16 * s + 16, 0:384]
        rs[s, 80:96, :] = g[16 * s:16 * s + 16, 384:768]
    cc = [
        remote(rs.at[2 * g + 1 - core], bc.at[g], gs.at[g], gr.at[g], c_peer) for g in range(8)
    ]
    start(cc)

    wait(wc3)
    for g in range(8):
        s1 = wl[g // 4, g % 4].reshape(256, E)
        s2 = wr[g // 4, g % 4].reshape(256, 384)
        rows = slice(96 * g, 96 * g + 96)
        w_full[0, rows] = moved(hot_s[0], s1, 1, 0)
        w_full[1, rows] = moved(hot_s[1], s1, 1, 0)
        w_full[2, rows] = moved(hot_s[2], s1, 1, 0)
        w_full[2, rows, 0:384] += moved(hot_s[3], s2, 1, 0)
        w_full[2, rows, 384:768] += moved(hot_s[4], s2, 1, 0)

    for g in range(8):
        cc[g].wait()
        acc1[g] = (rs[2 * g + core].astype(F32) + bc[g].astype(F32)).astype(BF)
    cz = []
    for s in range(1, 4):
        to = (z + s) % 4
        for q in range(2):
            k = 8 + (s - 1) * 2 + q
            cz.append(remote(acc1.at[q * 4 + to], bz.at[s - 1, q], gs.at[k], gr.at[k], z_peers[s - 1]))
    start(cz)

    local.wait()
    for kind in range(3):
        for s in range(1, ND):
            came(kind, (d + s) % ND).wait_recv()
    for s in range(1, ND):
        c = (d + s) % ND
        pl.when(c % 2 == half)(came(3, c).wait_recv)
    for k in range(4):
        lo, hi = 2 * k, 2 * k + 1
        sh = 2 * k + half
        for m in range(4):
            t_s[m, 192 * k:192 * k + 64] = b_buf[lo, 64 * m:64 * m + 64]
            t_s[m, 192 * k + 128:192 * k + 192] = b_buf[hi, 64 * m:64 * m + 64]
        for m in range(2):
            t_s[m, 192 * k + 64:192 * k + 128] = b_buf[sh, 384 + 64 * m:448 + 64 * m]
            rows = slice(256 + 64 * m, 320 + 64 * m)
            t_s[2 + m, 192 * k + 64:192 * k + 128] = (
                b_buf[lo, rows].astype(F32) + b_buf[hi, rows].astype(F32)
            ).astype(BF)

    wait(cz)
    for q in range(2):
        acc2[q] = (
            acc1[q * 4 + z].astype(F32)
            + bz[0, q].astype(F32)
            + bz[1, q].astype(F32)
            + bz[2, q].astype(F32)
        ).astype(BF)
    cx = remote(acc2.at[1 - xl], bx, gs.at[14], gr.at[14], x_peers[1])
    cx.start()
    out_ref[...] = (x_ref[...].astype(F32) + dot(t_s[0].T, w_full[3], 1, 0)).astype(BF)
    cx.wait()
    acc3[...] = acc2[xl].astype(F32) + bx[...].astype(F32)
    last = []
    for s in range(1, ND):
        to = (d + s) % ND
        rows = pl.ds(pl.multiple_of(to * 8, 8), 8)
        last.append(remote(acc3.at[rows], finq.at[d], gs.at[14 + s], gr.at[14 + s], depth_peers[s - 1]))
    partner = at(d + 1 - 2 * par, r)
    for k in range(2):
        rows = pl.ds(pl.multiple_of(64 + k * 16 + (1 - par) * 8, 8), 8)
        last.append(remote(acc3.at[rows], fino.at[k], gs.at[22 + k], gr.at[22 + k], partner))
    start(last)
    finq[d] = acc3[pl.ds(pl.multiple_of(d * 8, 8), 8), :]

    dn = dot(t_s[1].T, w_full[0], 1, 1)
    dn += dot(t_s[2].T, w_full[1], 1, 1)
    dn += dot(t_s[3].T, w_full[2], 1, 1)
    x = x_ref[...].astype(F32)
    centered = x - jnp.mean(x, axis=-1, keepdims=True)
    inverse = lax.rsqrt(jnp.mean(centered * centered, axis=-1, keepdims=True) + 1e-05)
    unit = centered * inverse
    du = dn * gain_ref[...]
    al_ref[...] = (
        u_ref[...].astype(F32)
        + inverse
        * (du - jnp.mean(du, axis=-1, keepdims=True) - unit * jnp.mean(du * unit, axis=-1, keepdims=True))
    ).astype(BF)

    wait(last)
    places = ((0, 320), (64, 192), (128, 256))
    dgain = jnp.zeros((6, 1), F32)
    for m, (g_ref, w_ref) in enumerate(((gq_ref, wq_ref), (gk_ref, wk_ref), (gv_ref, wv_ref))):
        own, sh = places[m]
        parts = []
        for k in range(4):
            parts.append(finq[2 * k, 0:6, own:own + 64])
            parts.append(finq[2 * k, 0:6, sh:sh + 64] + finq[2 * k + 1, 0:6, sh:sh + 64])
            parts.append(finq[2 * k + 1, 0:6, own:own + 64])
        g = jnp.concatenate(parts, axis=1)
        g_ref[...] = g
        dgain = dgain + jnp.sum(g * w_ref[...].astype(F32), axis=1, keepdims=True)
    for k in range(2):
        rows = pl.ds(pl.multiple_of(64 + k * 16 + par * 8, 8), 8)
        go_ref[:, k * 384:k * 384 + 384] = (acc3[rows, :] + fino[k])[0:6]
    F = lax.broadcasted_iota(jnp.int32, (6, E), 1)
    I = lax.broadcasted_iota(jnp.int32, (6, E), 0)
    own_gain = jnp.sum(
        jnp.where(F == 6 * (NR * d + r) + I, gain_ref[...], 0.0), axis=1, keepdims=True
    )
    dg_ref[...] = jnp.broadcast_to(dgain / own_gain, (6, 128))

    for kind in range(3):
        for s in range(1, ND):
            sent(kind, (d + s) % ND).wait_send()
    for i in range(4):
        c = 4 * par + i
        pl.when(c != d)(sent(3, c).wait_send)


def fused(x, u, gain, wq, wk, wv, we):
    vm = pl.BlockSpec(memory_space=pltpu.VMEM)
    dma = lambda *shape: pltpu.SemaphoreType.DMA(shape)
    grad = jax.ShapeDtypeStruct((6, E), F32)
    return pl.pallas_call(
        kernel,
        out_shape=(
            jax.ShapeDtypeStruct((ROWS, E), BF),
            jax.ShapeDtypeStruct((ROWS, E), BF),
            grad, grad, grad, grad,
            jax.ShapeDtypeStruct((6, 128), F32),
        ),
        in_specs=[vm] * 7,
        out_specs=(vm,) * 7,
        scratch_shapes=[
            pltpu.VMEM((ND, ROWS, E), BF),
            pltpu.VMEM((ND, ROWS, E), BF),
            pltpu.VMEM((2, 4, 2, 8, 16, E), BF),
            pltpu.VMEM((2, 4, 2, 8, 16, 384), BF),
            pltpu.VMEM((2, 4, 2, 8, 16, 256), BF),
            pltpu.VMEM((4, E, E), BF),
            pltpu.VMEM((7, 96, 256), BF),
            pltpu.VMEM((3, E, 128), BF),
            pltpu.VMEM((2, SEQ, HD), BF),
            pltpu.VMEM((2, SEQ, HD), BF),
            pltpu.VMEM((2, SEQ, HD), BF),
            pltpu.VMEM((2, SEQ, HD), BF),
            pltpu.VMEM((2, ND, HD, ROWS), BF),
            pltpu.VMEM((2, ND, HD, ROWS), BF),
            pltpu.VMEM((ND, ROWS, 128), BF),
            pltpu.VMEM((ND, ROWS, 128), BF),
            pltpu.VMEM((2, ND, 1, ROWS), F32),
            pltpu.VMEM((SEQ, ROWS), F32),
            pltpu.VMEM((SEQ, ROWS), F32),
            pltpu.VMEM((HD, SEQ), F32),
            pltpu.VMEM((HD, SEQ), F32),
            pltpu.VMEM((ND, 512, ROWS), BF),
            pltpu.VMEM((ND, 512, ROWS), BF),
            pltpu.VMEM((384, E), F32),
            pltpu.VMEM((128, E), F32),
            pltpu.VMEM((NR, 96, 384), BF),
            pltpu.VMEM((8, 96, 384), BF),
            pltpu.VMEM((8, 96, 384), BF),
            pltpu.VMEM((3, 2, 96, 384), BF),
            pltpu.VMEM((2, 96, 384), BF),
            pltpu.VMEM((96, 384), BF),
            pltpu.VMEM((96, 384), F32),
            pltpu.VMEM((ND, 8, 384), F32),
            pltpu.VMEM((2, 8, 384), F32),
            pltpu.VMEM((4, E, ROWS), BF),
            dma(9), dma(9), dma(9), dma(9), dma(33), dma(33), dma(7), dma(7),
            dma(4, ND), dma(4, ND), dma(24), dma(24), dma(3),
        ],
        compiler_params=pltpu.CompilerParams(
            collective_id=1, has_side_effects=True, vmem_limit_bytes=VMEM_LIMIT
        ),
        name="fused",
    )(x, u, gain, wq, wk, wv, we)


def body(x, gain, wq, wk, wv, we, u):
    out, al, gq, gk, gv, go, dg = fused(
        x.reshape(ROWS, E), u.reshape(ROWS, E), gain.reshape(1, E), wq, wk, wv, we
    )
    return out.reshape(ROWS, 1, E), al.reshape(ROWS, 1, E), gq, gk, gv, go, dg[:, 0]


def solution(mesh):
    rows = P("depth", "res", None)
    shard = P(("depth", "res"), None)
    return jax.shard_map(
        body,
        mesh=mesh,
        in_specs=(rows, P(), shard, shard, shard, shard, rows),
        out_specs=(rows, rows, shard, shard, shard, shard, P(("depth", "res"))),
        check_vma=False,
    )
```

time: 2020 us -> 138 us (0.07)
  waiting for transfers between devices: 979 us -> 0 us
  blocking collectives: 428 us -> 0 us
  starting transfers between devices: 354 us -> 0 us
  matrix products: 136 us -> 0 us
  Pallas kernels: 0 us -> 128 us
  local copies, waits for them, and re-layouts: 71.3 us -> 7.98 us
  other arithmetic: 22.2 us -> 0 us
    all_gather x6 -> x0, waiting for transfers between devices: 882 us -> none  [the longest x1 193 us: body(): lax.all_gather(lookup_weights, ('depth', 'res'), axis=0, tiled=True)]
    unnamed x2 -> x0, blocking collectives: 428 us -> none
    unnamed x128 -> x0, starting transfers between devices: 354 us -> none
    dot_general x84 -> x0, matrix products: 136 us -> none  [the longest x12 25.7 us: head_pass(): jnp.dot(probs_b, payload_entries, preferred_element_type=jnp.float32)]
    pallas_call x0 -> x1, Pallas kernels: none -> 128 us  [fused(): pl.pallas_call(kernel, out_shape=(jax.ShapeDtypeStruct((ROWS, E), BF), ja...]
    reduce_scatter x1 -> x0, waiting for transfers between devices: 91.9 us -> none  [body(): lax.psum_scatter(stacked, 'depth', scatter_dimension=0, tiled=True)]
    unnamed x239 -> x18, local copies, waits for them, and re-layouts: 61.6 us -> 6.08 us
  transfers between devices with their start and end apart: 135 -> 0, of which waited for: 9 -> 0; matrix products, arithmetic and copies ran while one was open for 4% -> 0% of each run, Pallas kernels for 0% -> 0%
where the time goes in v2:
time: 138 us; the launch traced here: 137 us
  Pallas kernels  128 us (93%)
  local copies, waits for them, and re-layouts  7.98 us (6%)
    pallas_call x1, Pallas kernels, fused(): pl.pallas_call(kernel, out_shape=(jax.ShapeDtypeStruct((ROWS, E), BF), ja...  128 us
    unnamed x18, local copies, waits for them, and re-layouts  6.08 us

profile of v2, /device:TPU:0, one launch (start us, length us, event | category | flops | bytes accessed | tf_op | source)
XLA Modules:
  0.0 136.7 jit_solution(18058309584524206899)
XLA Ops:
  0.6 1.3 reshape.31.gain_ref
  1.9 128.0 %fused.1 = (bf16[256,768]{1,0:T(8,128)(2,1)}, bf16[256,768]{1,0:T(8,128)(2,1)}, f32[6,768]{1,0:T(8,128)}, f32[6,768]{1,0:T(8,128)}, f32[6,768]{1,0:T(8,128)}, /*index=5*/f32[6,768]{1,0:T(8,128)}, f32[6,128]{1,0:T(8,128)}) custom-call(bf16[256,768]{1,0:T(8,128)(2,1)} %bitcast.4, bf16[256,768]{1,0:T(8,128)(2,1)} %bitcast.5, f32[1,768]{1,0:T(1,128)} %reshape.31.gain_ref, ...), custom_call_target="tpu_custom_call" | custom-call | tf_op jit(solution)/shard_map/fused/pallas_call | solution.py:529
  129.9 0.0 copy-start.5
  129.9 0.7 copy-done.5
  130.6 0.6 slice_reduce_fusion
  131.2 0.0 copy-start
  131.2 1.8 %copy.20 = bf16[256,1,768]{2,0,1:T(8,128)(2,1)} copy(bf16[256,1,768]{2,0,1:T(8,128)(2,1)} %bitcast.7) | data formatting | bytes 786432
  133.1 0.0 copy-done
  133.1 0.0 copy-start.4
  133.1 0.7 copy.21
  133.8 0.0 copy-done.4
  133.8 0.0 copy-start.3
  133.8 0.6 copy.22
  134.4 0.1 copy-done.3
  134.6 0.0 copy-start.2
  134.6 0.6 copy.23
  135.2 0.1 copy-done.2
  135.3 0.0 copy-start.1
  135.3 0.6 copy.24
  135.9 0.1 copy-done.1
  136.1 0.6 copy.25
Async XLA Ops:
  129.9 0.7 copy-start.5
  131.2 1.8 %copy-start = (bf16[256,768]{1,0:T(8,128)(2,1)S(1)}, bf16[256,768]{1,0:T(8,128)(2,1)}, u32[]{:S(2)}) copy-start(bf16[256,768]{1,0:T(8,128)(2,1)} %get-tuple-element.15) | copy-start | bytes 1179652
  133.1 0.8 copy-start.4
  133.8 0.7 copy-start.3
  134.6 0.7 copy-start.2
  135.3 0.7 copy-start.1

commit v3 on v2

v3 whole, which is shorter than its diff:
```python
import jax
import jax.numpy as jnp
from jax import lax
from jax.experimental import pallas as pl
from jax.experimental.pallas import tpu as pltpu
from jax.sharding import PartitionSpec as P

HD = 64
E = 768
ND = 8
NR = 16
ROWS = 256
SEQ = ND * ROWS
TILE = 256
SCALE = HD ** (-0.5)
MESH = pl.DeviceIdType.MESH
BF = jnp.bfloat16
F32 = jnp.float32
VMEM_LIMIT = 58 * 1024 * 1024


def place():
    d = lax.axis_index("depth")
    r = lax.axis_index("res")
    return d, r, d // 4, d % 4, r // 8, (r // 2) % 4, r % 2


def at(d, r):
    return {"depth": d, "res": r}


def barrier(peers):
    sem = pltpu.get_barrier_semaphore()
    for peer in peers:
        pl.semaphore_signal(sem, inc=1, device_id=peer, device_id_type=MESH)
    pl.semaphore_wait(sem, len(peers))


def remote(src, dst, send, recv, peer):
    return pltpu.make_async_remote_copy(
        src_ref=src, dst_ref=dst, send_sem=send, recv_sem=recv, device_id=peer, device_id_type=MESH
    )


def start(copies):
    for c in copies:
        c.start()


def wait(copies):
    for c in copies:
        c.wait()


def dot(a, b, ca, cb):
    return lax.dot_general(a, b, (((ca,), (cb,)), ((), ())), preferred_element_type=F32)


def hot(mask):
    return jnp.where(mask, 1.0, 0.0).astype(BF)


def moved(a, b, ca, cb):
    return dot(a, b, ca, cb).astype(BF)


SPLIT = 64
KINDS = ((0, 64), (64, 128), (128, 192), (192, 320), (320, 448), (448, 512))


def ring(full, d, xh, y, r, ss, rs):
    e = (d + 4) % ND
    across, up, down = at(e, r), at(xh * 4 + (y + 1) % 4, r), at(xh * 4 + (y + 3) % 4, r)
    lo, hi, far = xh * 4 + (y + 3) % 4, xh * 4 + (y + 1) % 4, xh * 4 + (y + 2) % 4
    mid = SPLIT + 96

    def send(k, peer, block, rows):
        return remote(full.at[block, rows], full.at[block, rows], ss.at[k], rs.at[k], peer)

    whole = slice(0, ROWS)
    c0 = send(0, across, d, whole)
    near = (send(1, up, d, whole), send(2, down, d, whole))
    near2 = (send(3, up, e, slice(SPLIT, ROWS)), send(4, down, e, slice(SPLIT, ROWS)))
    on = (send(5, up, lo, slice(0, 128)), send(6, down, hi, slice(128, ROWS)))
    cross = (send(7, across, lo, slice(0, SPLIT)), send(8, across, hi, slice(0, SPLIT)))
    cross2 = (send(9, across, far, slice(0, SPLIT)),)
    lo2, hi2 = (lo + 4) % ND, (hi + 4) % ND
    on2 = (send(10, up, lo2, slice(SPLIT, mid)), send(11, down, hi2, slice(mid, ROWS)))
    return c0, near, near2, on, cross, cross2, on2


def kernel(
    x_hbm, u_hbm, gain_ref, wq_ref, wk_ref, wv_ref, we_ref,
    out_hbm, al_hbm, gq_ref, gk_ref, gv_ref, go_ref, dg_ref,
    x_ref, u_ref, out_ref, al_ref, n_all, wl, wr, wc, w_full, hot_s, sel_s, perm_g, perm_o,
    q_s, k_s, v_s, a_s, kt_s, vt_s, a_out, a_in, lse_s, p_s, dp_s, dk_s, dv_s,
    p_buf, b_buf, gt_s, rs, bc, acc1, bz, acc2, bx, acc3, finq, t_s,
    ro, boc, oc, boz, ox, box, oy, boy,
    ns, nr, ws, wrs, as_, ar, ps, pr, gs, gr, os_, or_, loc,
):
    d, r, xh, y, xl, z, core = place()
    par, j, half = d % 2, d // 2, d // 4
    zc = z * 2 + core
    depth_peers = [at((d + s) % ND, r) for s in range(1, ND)]
    y_peers = [at(xh * 4 + (y + s) % 4, r) for s in range(1, 4)]
    x_peers = [at((1 - xh) * 4 + y, r), at(d, (1 - xl) * 8 + zc), at((1 - xh) * 4 + y, (1 - xl) * 8 + zc)]
    z_peers = [at(d, xl * 8 + ((z + s) % 4) * 2 + core) for s in range(1, 4)]
    z_from = [((z + 4 - s) % 4) * 2 + core for s in range(1, 4)]
    c_peer = at(d, xl * 8 + z * 2 + 1 - core)
    x_in = pltpu.make_async_copy(x_hbm, x_ref, loc.at[3])
    u_in = pltpu.make_async_copy(u_hbm, u_ref, loc.at[4])
    x_in.start()
    u_in.start()
    barrier(depth_peers + x_peers[1:] + z_peers + [c_peer])

    top = jnp.concatenate(
        [wq_ref[...].astype(F32), wk_ref[...].astype(F32), wv_ref[0:4].astype(F32)], axis=0
    )
    rest = jnp.concatenate([wv_ref[4:6].astype(F32), we_ref[...].astype(F32)], axis=0)
    rest = jnp.concatenate([rest[:, 0:384], rest[:, 384:768]], axis=0)
    wl[xh, y, xl, zc] = top.astype(BF)
    wr[xh, y, xl, zc] = rest.astype(BF)
    wy = []
    for s in range(3):
        for k, w in enumerate((wl, wr)):
            one = w.at[xh, y, xl, zc]
            wy.append(remote(one, one, ws.at[2 * s + k], wrs.at[2 * s + k], y_peers[s]))
    start(wy)

    x_in.wait()
    gain = gain_ref[...].reshape(1, E)
    x = x_ref[...].astype(F32)
    centered = x - jnp.mean(x, axis=-1, keepdims=True)
    inverse = lax.rsqrt(jnp.mean(centered * centered, axis=-1, keepdims=True) + 1e-05)
    n_all[d] = (centered * inverse * gain).astype(BF)
    n0, n_near, n_near2, n_on, n_cross, n_cross2, n_on2 = ring(n_all, d, xh, y, r, ns, nr)
    n0.start()

    window = pl.multiple_of(128 * ((3 * j) // 2), 128)
    offset = 192 * j - 128 * ((3 * j) // 2)
    other = pl.multiple_of(128 * ((3 * (2 * (1 - xh) + y // 2)) // 2), 128)
    wait(wy)
    start(n_near)
    windows = (other, window, other)
    wx = []
    for s in range(3):
        mine = wl.at[xh, :, xl, zc, :, pl.ds(windows[s], 256)]
        wx.append(remote(mine, wc.at[xh, :, xl, zc], ws.at[6 + 2 * s], wrs.at[6 + 2 * s], x_peers[s]))
        slab = wr.at[xh, :, xl, zc]
        wx.append(remote(slab, slab, ws.at[7 + 2 * s], wrs.at[7 + 2 * s], x_peers[s]))
    start(wx)
    own_w = pltpu.make_async_copy(
        wl.at[xh, :, xl, zc, :, pl.ds(window, 256)], wc.at[xh, :, xl, zc], loc.at[1]
    )
    own_w.start()
    R = lax.broadcasted_iota(jnp.int32, (96, 256), 0)
    K = lax.broadcasted_iota(jnp.int32, (96, 256), 1)
    o16, i6 = 16 * (R // 6), R % 6
    hot_s[0] = hot(K == o16 + i6)
    hot_s[1] = hot(K == o16 + 6 + i6)
    hot_s[2] = hot((K == o16 + 12 + i6) & (i6 < 4))
    hot_s[3] = hot((K == o16 + i6 - 4) & (i6 >= 4))
    hot_s[4] = hot((K == o16 + 8 + i6 - 4) & (i6 >= 4))
    hot_s[5] = hot(K == o16 + 2 + i6)
    hot_s[6] = hot(K == o16 + 10 + i6)
    K2 = lax.broadcasted_iota(jnp.int32, (256, 128), 0)
    C2 = lax.broadcasted_iota(jnp.int32, (256, 128), 1)
    pick = hot(K2 == jnp.where(C2 < 64, offset + 128 * par + C2, offset + C2))
    n0.wait()
    start(n_near2)
    wait(wx)
    own_w.wait()

    slab = wc.at[:, :, :, zc]
    wz1 = [remote(slab, slab, ws.at[12 + s], wrs.at[12 + s], z_peers[s]) for s in range(3)]
    start(wz1)
    wc1 = [remote(slab, slab, ws.at[15], wrs.at[15], c_peer)]
    start(wc1)
    slab = wr.at[:, :, :, zc]
    wz2 = [remote(slab, slab, ws.at[19 + s], wrs.at[19 + s], z_peers[s]) for s in range(3)]
    start(wz2)
    wc2 = [remote(slab, slab, ws.at[22], wrs.at[22], c_peer)]
    start(wc2)
    wait(n_near)
    start(n_on)
    start(n_cross)
    slab = wl.at[xh, :, xl, zc]
    wx2 = [remote(slab, slab, ws.at[33 + s], wrs.at[33 + s], x_peers[s]) for s in range(3)]
    start(wx2)
    p_buf[:, 448:512, :] = jnp.zeros((ND, 64, ROWS), BF)

    def orders(b, _):
        R = lax.broadcasted_iota(jnp.int32, (64, E), 0)
        F = lax.broadcasted_iota(jnp.int32, (64, E), 1)
        i = R % 8
        owner = 16 * ((R // 8) % 8) + 2 * (b % 8) + b // 8
        perm_g[b // 8, b % 8] = hot((F == 6 * owner + i) & (i < 6))
        return 0

    lax.fori_loop(0, NR, orders, 0)

    def orders_o(b, _):
        R = lax.broadcasted_iota(jnp.int32, (96, E), 0)
        F = lax.broadcasted_iota(jnp.int32, (96, E), 1)
        q = R // 24
        owner = (((q // 2) * 4 + (R // 6) % 4) * 2 + q % 2) * 8 + (b % 4) * 2 + b // 4
        perm_o[b] = hot(F == 6 * owner + R % 6)
        return 0

    lax.fori_loop(0, 8, orders_o, 0)

    for s in range(3):
        wz1[s].wait()
        there = wc.at[:, :, :, z_from[s]]
        c = remote(there, there, ws.at[16 + s], wrs.at[16 + s], c_peer)
        c.start()
        wc1.append(c)
    wait(n_near2)
    start(n_on2)
    wait(n_on)
    start(n_cross2)
    wait(wc1)

    for g in range(8):
        s1 = moved(wc[g // 4, g % 4].reshape(256, 256), pick, 1, 0)
        rows = slice(96 * g, 96 * g + 96)
        for m in range(3):
            sel_s[rows, 128 * m:128 * m + 128] = moved(hot_s[m], s1, 1, 0)

    for s in range(3):
        wz2[s].wait()
        there = wr.at[:, :, :, z_from[s]]
        c = remote(there, there, ws.at[23 + s], wrs.at[23 + s], c_peer)
        c.start()
        wc2.append(c)
    wait(wx2)
    slab = wl.at[:, :, :, zc]
    wz3 = [remote(slab, slab, ws.at[26 + s], wrs.at[26 + s], z_peers[s]) for s in range(3)]
    start(wz3)
    wc3 = [remote(slab, slab, ws.at[29], wrs.at[29], c_peer)]
    start(wc3)
    wait(wc2)
    u_in.wait()
    for g in range(8):
        s2 = wr[g // 4, g % 4].reshape(256, 384)
        rows = slice(96 * g, 96 * g + 96)
        w_full[3, rows, 0:384] = moved(hot_s[5], s2, 1, 0)
        w_full[3, rows, 384:768] = moved(hot_s[6], s2, 1, 0)
    a = dot(u_ref[...], w_full[3], 1, 1).astype(BF)
    for t in range(ND):
        own, sh = 192 * (t // 2) + 128 * (t % 2), 192 * (t // 2) + 64
        a_out[t] = jnp.concatenate([a[:, own:own + HD], a[:, sh:sh + HD]], axis=1)
    ca = []
    for s in range(1, ND):
        c = remote(a_out.at[(d + s) % ND], a_in.at[d], as_.at[s - 1], ar.at[s - 1], depth_peers[s - 1])
        c.start()
        ca.append(c)
    a_in[d] = a_out[d]

    inner = pl.multiple_of(128 * ((3 * j) // 2) - 384 * half, 128)
    for g in range(8):
        s2 = moved(wr[g // 4, g % 4, :, :, :, pl.ds(inner, 256)].reshape(256, 256), pick, 1, 0)
        late = jnp.where(half == 0, hot_s[3], hot_s[4])
        rows = slice(96 * g, 96 * g + 96)
        sel_s[rows, 256:384] = sel_s[rows, 256:384] + moved(late, s2, 1, 0)

    def project(i, group):
        c = group * 4 + (y + i) % 4
        rows = pl.ds(pl.multiple_of(c * ROWS, ROWS), ROWS)
        qkv = dot(n_all[c], sel_s[...], 1, 0)
        q = (SCALE * qkv[:, 0:128]).astype(BF)
        k = qkv[:, 128:256].astype(BF)
        v = qkv[:, 256:384].astype(BF)
        kt = k.T
        vt = v.T
        for h in range(2):
            q_s[h, rows, :] = q[:, h * HD:h * HD + HD]
            k_s[h, rows, :] = k[:, h * HD:h * HD + HD]
            v_s[h, rows, :] = v[:, h * HD:h * HD + HD]
            kt_s[h, c] = kt[h * HD:h * HD + HD]
            vt_s[h, c] = vt[h * HD:h * HD + HD]
        return group

    lax.fori_loop(0, 4, project, xh)
    wait(n_on2)
    wait(n_cross)
    wait(n_cross2)
    lax.fori_loop(0, 4, project, 1 - xh)

    def sent(kind, c):
        rows = slice(*KINDS[kind])
        return remote(
            p_buf.at[c, rows], b_buf.at[d, rows], ps.at[kind, c], pr.at[kind, d], at(c, r)
        )

    def came(kind, c):
        rows = slice(*KINDS[kind])
        return remote(
            p_buf.at[c, rows], b_buf.at[c, rows], ps.at[kind, c], pr.at[kind, c], at(c, r)
        )

    def forward(h, c):
        q = q_s[h, pl.ds(pl.multiple_of(c * ROWS, ROWS), ROWS), :]
        m = jnp.full((8, ROWS), -jnp.inf, F32)
        for t in range(SEQ // TILE):
            ts = slice(t * TILE, t * TILE + TILE)
            s = dot(k_s[h, ts, :], q, 1, 1)
            p_s[ts, :] = s
            m = jnp.maximum(m, jnp.max(s.reshape(TILE // 8, 8, ROWS), axis=0))
        m = jnp.max(m, axis=0, keepdims=True)
        l = jnp.zeros((8, ROWS), F32)
        att = jnp.zeros((HD, ROWS), F32)
        for t in range(SEQ // TILE):
            e = jnp.exp(p_s[t * TILE:t * TILE + TILE, :] - m)
            l = l + jnp.sum(e.reshape(TILE // 8, 8, ROWS), axis=0)
            att += dot(vt_s[h, t], e.astype(BF), 1, 0)
        l = jnp.sum(l, axis=0, keepdims=True)
        p_buf[c, h * HD:h * HD + HD, :] = (att * (1.0 / l)).astype(BF)
        lse_s[h, c] = m + jnp.log(l)
        pl.when(c != d)(lambda: sent(h, c).start())

    def forward_shared(i, _):
        forward(1, 4 * par + i)
        return 0

    def forward_own(i, _):
        forward(0, i)
        return 0

    lax.fori_loop(0, 4, forward_shared, 0)
    lax.fori_loop(0, 8, forward_own, 0)
    local = pltpu.make_async_copy(p_buf.at[d, 0:128], b_buf.at[d, 0:128], loc.at[0])
    local.start()
    wait(ca)

    def spread(c, _):
        rows = pl.ds(pl.multiple_of(c * ROWS, ROWS), ROWS)
        got = a_in[c]
        a_s[0, rows, :] = got[:, 0:HD]
        a_s[1, rows, :] = got[:, HD:2 * HD]
        return 0

    lax.fori_loop(0, ND, spread, 0)
    for s in range(3):
        wz3[s].wait()
        there = wl.at[:, :, :, z_from[s]]
        c = remote(there, there, ws.at[30 + s], wrs.at[30 + s], c_peer)
        c.start()
        wc3.append(c)

    def attend(h, c, base):
        rows = pl.ds(pl.multiple_of(c * ROWS, ROWS), ROWS)
        q = q_s[h, rows, :]
        a = a_s[h, rows, :]
        qt, at_ = q.T, a.T
        lse = lse_s[h, c]
        delta = jnp.zeros((8, ROWS), F32)
        for t in range(SEQ // TILE):
            ts = slice(t * TILE, t * TILE + TILE)
            p = jnp.exp(dot(k_s[h, ts, :], q, 1, 1) - lse)
            dp = dot(v_s[h, ts, :], a, 1, 1)
            p_s[ts, :] = p
            dp_s[ts, :] = dp
            delta = delta + jnp.sum((p * dp).reshape(TILE // 8, 8, ROWS), axis=0)
        delta = jnp.sum(delta, axis=0, keepdims=True)
        dq = jnp.zeros((HD, ROWS), F32)
        for t in range(SEQ // TILE):
            ts = slice(t * TILE, t * TILE + TILE)
            p = p_s[ts, :]
            pb = p.astype(BF)
            ds = (p * (dp_s[ts, :] - delta)).astype(BF)
            dq += dot(kt_s[h, t], ds, 1, 0)
            dk_s[:, ts] += dot(qt, ds, 1, 1)
            dv_s[:, ts] += dot(at_, pb, 1, 1)
        p_buf[c, base:base + HD, :] = (SCALE * dq).astype(BF)

    def totals(base, kind):
        for c in range(ND):
            cols = slice(c * ROWS, c * ROWS + ROWS)
            p_buf[c, base:base + HD, :] = dk_s[:, cols].astype(BF)
            p_buf[c, base + HD:base + 2 * HD, :] = dv_s[:, cols].astype(BF)
        for s in range(1, ND):
            sent(kind, (d + s) % ND).start()

    def attend_shared(i, _):
        c = 4 * par + i
        attend(1, c, 448)
        pl.when(c != d)(lambda: sent(5, c).start())
        return 0

    def attend_own(c, _):
        attend(0, c, 128)
        pl.when(c != d)(lambda: sent(2, c).start())
        return 0

    def grads(h):
        rows = slice(128, 320) if h == 0 else slice(320, 512)
        for t in range(3):
            cols = slice(256 * t, 256 * t + 256)
            total = dot(p_buf[0, rows], n_all[0, :, cols], 1, 0)
            for c in range(1, ND):
                total += dot(p_buf[c, rows], n_all[c, :, cols], 1, 0)
            gt_s[:, cols] = total.astype(BF)
        for b in range(2):
            rs[h, b] = moved(perm_g[b].reshape(512, E), gt_s[...], 1, 1).reshape(8, 64, 192)

    def sum_cores(h, copies):
        for g in range(8):
            copies[g].wait()
            acc1[h, g] = (rs[h, core, g].astype(F32) + bc[h, g].astype(F32)).astype(BF)
        out = []
        for s in range(1, 4):
            for q in range(2):
                k = 8 + (s - 1) * 2 + q
                to = acc1.at[h, q * 4 + (z + s) % 4]
                out.append(remote(to, bz.at[h, s - 1, q], gs.at[h, k], gr.at[h, k], z_peers[s - 1]))
        start(out)
        return out

    def sum_z(h, copies):
        wait(copies)
        for q in range(2):
            acc2[h, q] = (
                acc1[h, q * 4 + z].astype(F32)
                + bz[h, 0, q].astype(F32)
                + bz[h, 1, q].astype(F32)
                + bz[h, 2, q].astype(F32)
            ).astype(BF)
        out = remote(acc2.at[h, 1 - xl], bx.at[h], gs.at[h, 14], gr.at[h, 14], x_peers[1])
        out.start()
        return out

    def sum_x(h, copy):
        copy.wait()
        acc3[h] = acc2[h, xl].astype(F32) + bx[h].astype(F32)
        out = []
        for s in range(1, ND):
            rows = pl.ds(pl.multiple_of(((d + s) % ND) * 8, 8), 8)
            out.append(
                remote(acc3.at[h, rows], finq.at[h, d], gs.at[h, 14 + s], gr.at[h, 14 + s], depth_peers[s - 1])
            )
        start(out)
        finq[h, d] = acc3[h, pl.ds(pl.multiple_of(d * 8, 8), 8), :]
        return out

    dk_s[...] = jnp.zeros_like(dk_s)
    dv_s[...] = jnp.zeros_like(dv_s)
    lax.fori_loop(0, 4, attend_shared, 0)
    totals(320, 4)
    grads(1)
    sc = [
        remote(rs.at[1, 1 - core, g], bc.at[1, g], gs.at[1, g], gr.at[1, g], c_peer) for g in range(8)
    ]
    start(sc)

    local.wait()
    for s in range(1, ND):
        c = (d + s) % ND
        came(0, c).wait_recv()
        pl.when(c % 2 == half)(came(1, c).wait_recv)
    for k in range(4):
        t_s[0, 192 * k:192 * k + 64] = b_buf[2 * k, 0:64]
        t_s[0, 192 * k + 64:192 * k + 128] = b_buf[2 * k + half, 64:128]
        t_s[0, 192 * k + 128:192 * k + 192] = b_buf[2 * k + 1, 0:64]
    out_ref[...] = (x_ref[...].astype(F32) + dot(t_s[0].T, w_full[3], 1, 0)).astype(BF)
    out_copy = pltpu.make_async_copy(out_ref, out_hbm, loc.at[5])
    out_copy.start()
    go = dot(t_s[0], u_ref[...], 1, 0).astype(BF)
    for k in range(8):
        ro[k // 4, k % 4] = moved(perm_o[k], go, 1, 0)
    oc_copies = [
        remote(ro.at[1 - core, k], boc.at[k], os_.at[k], or_.at[k], c_peer) for k in range(4)
    ]
    start(oc_copies)

    dk_s[...] = jnp.zeros_like(dk_s)
    dv_s[...] = jnp.zeros_like(dv_s)
    lax.fori_loop(0, 2, attend_own, 0)
    for k in range(4):
        oc_copies[k].wait()
        oc[k] = (ro[core, k].astype(F32) + boc[k].astype(F32)).astype(BF)
    oz_copies = [
        remote(oc.at[(z + s) % 4], boz.at[s - 1], os_.at[3 + s], or_.at[3 + s], z_peers[s - 1])
        for s in range(1, 4)
    ]
    start(oz_copies)
    sz = sum_cores(1, sc)
    lax.fori_loop(2, 5, attend_own, 0)
    wait(oz_copies)
    total = (
        oc[z].astype(F32) + boz[0].astype(F32) + boz[1].astype(F32) + boz[2].astype(F32)
    )
    gap = jnp.zeros((2, E), F32)
    for q in range(4):
        parts = []
        for t in range(4):
            parts += [total[24 * q + 6 * t:24 * q + 6 * t + 6], gap]
        ox[q] = jnp.concatenate(parts, axis=0).astype(BF)
    x_to = [(1 - xh) * 2 + xl, xh * 2 + 1 - xl, (1 - xh) * 2 + 1 - xl]
    ox_copies = [
        remote(ox.at[x_to[s]], box.at[s], os_.at[7 + s], or_.at[7 + s], x_peers[s]) for s in range(3)
    ]
    start(ox_copies)
    sx = sum_z(1, sz)
    lax.fori_loop(5, 7, attend_own, 0)
    wait(ox_copies)
    total = (
        ox[xh * 2 + xl].astype(F32) + box[0].astype(F32) + box[1].astype(F32) + box[2].astype(F32)
    )
    for t in range(4):
        oy[t] = total[8 * t:8 * t + 8]
    oy_copies = [
        remote(oy.at[(y + s) % 4], boy.at[s - 1], os_.at[9 + s], or_.at[9 + s], y_peers[s - 1])
        for s in range(1, 4)
    ]
    start(oy_copies)
    sd = sum_x(1, sx)
    lax.fori_loop(7, 8, attend_own, 0)
    totals(192, 3)
    local = pltpu.make_async_copy(p_buf.at[d, 128:512], b_buf.at[d, 128:512], loc.at[2])
    local.start()

    grads(0)
    cc = [
        remote(rs.at[0, 1 - core, g], bc.at[0, g], gs.at[0, g], gr.at[0, g], c_peer) for g in range(8)
    ]
    start(cc)

    wait(wc3)
    for g in range(8):
        s1 = wl[g // 4, g % 4].reshape(256, E)
        s2 = wr[g // 4, g % 4].reshape(256, 384)
        rows = slice(96 * g, 96 * g + 96)
        w_full[0, rows] = moved(hot_s[0], s1, 1, 0)
        w_full[1, rows] = moved(hot_s[1], s1, 1, 0)
        w_full[2, rows] = moved(hot_s[2], s1, 1, 0)
        w_full[2, rows, 0:384] += moved(hot_s[3], s2, 1, 0)
        w_full[2, rows, 384:768] += moved(hot_s[4], s2, 1, 0)

    cz = sum_cores(0, cc)

    local.wait()
    for s in range(1, ND):
        c = (d + s) % ND
        for kind in (2, 3, 4):
            came(kind, c).wait_recv()
        pl.when(c % 2 == half)(came(5, c).wait_recv)
    for k in range(4):
        lo, hi = 2 * k, 2 * k + 1
        for m in range(3):
            rows = slice(128 + 64 * m, 192 + 64 * m)
            t_s[1 + m, 192 * k:192 * k + 64] = b_buf[lo, rows]
            t_s[1 + m, 192 * k + 128:192 * k + 192] = b_buf[hi, rows]
        t_s[1, 192 * k + 64:192 * k + 128] = b_buf[lo + half, 448:512]
        for m in range(2):
            rows = slice(320 + 64 * m, 384 + 64 * m)
            t_s[2 + m, 192 * k + 64:192 * k + 128] = (
                b_buf[lo, rows].astype(F32) + b_buf[hi, rows].astype(F32)
            ).astype(BF)

    cx = sum_z(0, cz)
    dn = dot(t_s[1].T, w_full[0], 1, 1)
    dn += dot(t_s[2].T, w_full[1], 1, 1)
    dn += dot(t_s[3].T, w_full[2], 1, 1)
    last = sum_x(0, cx)
    x = x_ref[...].astype(F32)
    centered = x - jnp.mean(x, axis=-1, keepdims=True)
    inverse = lax.rsqrt(jnp.mean(centered * centered, axis=-1, keepdims=True) + 1e-05)
    unit = centered * inverse
    du = dn * gain
    al_ref[...] = (
        u_ref[...].astype(F32)
        + inverse
        * (du - jnp.mean(du, axis=-1, keepdims=True) - unit * jnp.mean(du * unit, axis=-1, keepdims=True))
    ).astype(BF)

    al_copy = pltpu.make_async_copy(al_ref, al_hbm, loc.at[6])
    al_copy.start()

    wait(sd)
    wait(last)
    places = ((0, 128), (64, 0), (128, 64))
    dgain = jnp.zeros((6, 1), F32)
    for m, (g_ref, w_ref) in enumerate(((gq_ref, wq_ref), (gk_ref, wk_ref), (gv_ref, wv_ref))):
        own, sh = places[m]
        parts = []
        for k in range(4):
            parts.append(finq[0, 2 * k, 0:6, own:own + 64])
            parts.append(finq[1, 2 * k, 0:6, sh:sh + 64] + finq[1, 2 * k + 1, 0:6, sh:sh + 64])
            parts.append(finq[0, 2 * k + 1, 0:6, own:own + 64])
        g = jnp.concatenate(parts, axis=1)
        g_ref[...] = g
        dgain = dgain + jnp.sum(g * w_ref[...].astype(F32), axis=1, keepdims=True)
    wait(oy_copies)
    go_ref[...] = (oy[y] + boy[0] + boy[1] + boy[2])[0:6]
    F = lax.broadcasted_iota(jnp.int32, (6, E), 1)
    I = lax.broadcasted_iota(jnp.int32, (6, E), 0)
    own_gain = jnp.sum(
        jnp.where(F == 6 * (NR * d + r) + I, gain, 0.0), axis=1, keepdims=True
    )
    dg_ref[0:6] = jnp.broadcast_to(dgain / own_gain, (6, 128))
    dg_ref[6:8] = jnp.zeros((2, 128), F32)

    out_copy.wait()
    al_copy.wait()
    for s in range(1, ND):
        for kind in (0, 2, 3, 4):
            sent(kind, (d + s) % ND).wait_send()
    for i in range(4):
        c = 4 * par + i
        for kind in (1, 5):
            pl.when(c != d)(sent(kind, c).wait_send)


def fused(x, u, gain, wq, wk, wv, we):
    vm = pl.BlockSpec(memory_space=pltpu.VMEM)
    hbm = pl.BlockSpec(memory_space=pl.ANY)
    dma = lambda *shape: pltpu.SemaphoreType.DMA(shape)
    grad = jax.ShapeDtypeStruct((6, E), F32)
    return pl.pallas_call(
        kernel,
        out_shape=(
            jax.ShapeDtypeStruct((ROWS, E), BF),
            jax.ShapeDtypeStruct((ROWS, E), BF),
            grad, grad, grad, grad,
            jax.ShapeDtypeStruct((8, 128), F32),
        ),
        in_specs=[hbm] * 2 + [vm] * 5,
        out_specs=(hbm, hbm) + (vm,) * 5,
        scratch_shapes=[
            pltpu.VMEM((ROWS, E), BF),
            pltpu.VMEM((ROWS, E), BF),
            pltpu.VMEM((ROWS, E), BF),
            pltpu.VMEM((ROWS, E), BF),
            pltpu.VMEM((ND, ROWS, E), BF),
            pltpu.VMEM((2, 4, 2, 8, 16, E), BF),
            pltpu.VMEM((2, 4, 2, 8, 16, 384), BF),
            pltpu.VMEM((2, 4, 2, 8, 16, 256), BF),
            pltpu.VMEM((4, E, E), BF),
            pltpu.VMEM((7, 96, 256), BF),
            pltpu.VMEM((E, 384), BF),
            pltpu.VMEM((2, 8, 64, E), BF),
            pltpu.VMEM((8, 96, E), BF),
            pltpu.VMEM((2, SEQ, HD), BF),
            pltpu.VMEM((2, SEQ, HD), BF),
            pltpu.VMEM((2, SEQ, HD), BF),
            pltpu.VMEM((2, SEQ, HD), BF),
            pltpu.VMEM((2, ND, HD, ROWS), BF),
            pltpu.VMEM((2, ND, HD, ROWS), BF),
            pltpu.VMEM((ND, ROWS, 128), BF),
            pltpu.VMEM((ND, ROWS, 128), BF),
            pltpu.VMEM((2, ND, 1, ROWS), F32),
            pltpu.VMEM((SEQ, ROWS), F32),
            pltpu.VMEM((SEQ, ROWS), F32),
            pltpu.VMEM((HD, SEQ), F32),
            pltpu.VMEM((HD, SEQ), F32),
            pltpu.VMEM((ND, 512, ROWS), BF),
            pltpu.VMEM((ND, 512, ROWS), BF),
            pltpu.VMEM((192, E), BF),
            pltpu.VMEM((2, 2, 8, 64, 192), BF),
            pltpu.VMEM((2, 8, 64, 192), BF),
            pltpu.VMEM((2, 8, 64, 192), BF),
            pltpu.VMEM((2, 3, 2, 64, 192), BF),
            pltpu.VMEM((2, 2, 64, 192), BF),
            pltpu.VMEM((2, 64, 192), BF),
            pltpu.VMEM((2, 64, 192), F32),
            pltpu.VMEM((2, ND, 8, 192), F32),
            pltpu.VMEM((4, E, ROWS), BF),
            pltpu.VMEM((2, 4, 96, E), BF),
            pltpu.VMEM((4, 96, E), BF),
            pltpu.VMEM((4, 96, E), BF),
            pltpu.VMEM((3, 96, E), BF),
            pltpu.VMEM((4, 32, E), BF),
            pltpu.VMEM((3, 32, E), BF),
            pltpu.VMEM((4, 8, E), F32),
            pltpu.VMEM((3, 8, E), F32),
            dma(12), dma(12), dma(36), dma(36), dma(7), dma(7),
            dma(6, ND), dma(6, ND), dma(2, 22), dma(2, 22), dma(13), dma(13), dma(7),
        ],
        compiler_params=pltpu.CompilerParams(
            collective_id=1, has_side_effects=True, vmem_limit_bytes=VMEM_LIMIT
        ),
        name="fused",
    )(x, u, gain, wq, wk, wv, we)


def finish_kernel(*refs):
    for k in range(6):
        refs[7 + k][...] = refs[k][...]
    refs[13][...] = refs[6][...].T[0, 0:6]


def finish(arrays):
    vm = pl.BlockSpec(memory_space=pltpu.VMEM)
    return pl.pallas_call(
        finish_kernel,
        out_shape=tuple(jax.ShapeDtypeStruct(a.shape, a.dtype) for a in arrays[:6])
        + (jax.ShapeDtypeStruct((6,), F32),),
        in_specs=[vm] * 7,
        out_specs=(vm,) * 7,
        name="finish",
    )(*arrays)


def body(x, gain, wq, wk, wv, we, u):
    out, al, gq, gk, gv, go, dg = finish(
        fused(x.reshape(ROWS, E), u.reshape(ROWS, E), gain, wq, wk, wv, we)
    )
    return out.reshape(ROWS, 1, E), al.reshape(ROWS, 1, E), gq, gk, gv, go, dg


def solution(mesh):
    rows = P("depth", "res", None)
    shard = P(("depth", "res"), None)
    return jax.shard_map(
        body,
        mesh=mesh,
        in_specs=(rows, P(), shard, shard, shard, shard, rows),
        out_specs=(rows, rows, shard, shard, shard, shard, P(("depth", "res"))),
        check_vma=False,
    )
```

time: 138 us -> 118 us (0.86); the launches traced: 137 us -> 118 us
  Pallas kernels: 128 us -> 118 us
  local copies, waits for them, and re-layouts: 7.98 us -> 0 us
    pallas_call x1, Pallas kernels: 128 us -> 116 us  [fused(): pl.pallas_call(kernel, out_shape=(jax.ShapeDtypeStruct((ROWS, E), BF), ja...]
    unnamed x18 -> x0, local copies, waits for them, and re-layouts: 6.08 us -> none
    pallas_call x0 -> x1, Pallas kernels: none -> 2.08 us  [finish(): pl.pallas_call(finish_kernel, out_shape=tuple((jax.ShapeDtypeStruct(a.sha...]
where the time goes in v3:
time: 118 us
  Pallas kernels  118 us (100%)
    pallas_call x1, Pallas kernels, fused(): pl.pallas_call(kernel, out_shape=(jax.ShapeDtypeStruct((ROWS, E), BF), ja...  116 us

profile of v3, /device:TPU:0, one launch (start us, length us, event | category | flops | bytes accessed | tf_op | source)
XLA Modules:
  0.0 118.3 jit_solution(12084672115901302921)
XLA Ops:
  0.6 115.5 %fused.1 = (bf16[256,768]{1,0:T(8,128)(2,1)}, bf16[256,768]{1,0:T(8,128)(2,1)}, f32[6,768]{1,0:T(8,128)}, f32[6,768]{1,0:T(8,128)}, f32[6,768]{1,0:T(8,128)}, /*index=5*/f32[6,768]{1,0:T(8,128)}, f32[8,128]{1,0:T(8,128)}) custom-call(bf16[256,768]{1,0:T(8,128)(2,1)} %bitcast.4, bf16[256,768]{1,0:T(8,128)(2,1)} %bitcast.5, f32[768]{0:T(1024)} %gain_ref.1, ...), custom_call_target="tpu_custom_call" | custom-call | tf_op jit(solution)/shard_map/fused/pallas_call | solution.py:620
  116.2 2.1 %finish.1 = (bf16[256,768]{1,0:T(8,128)(2,1)}, bf16[256,768]{1,0:T(8,128)(2,1)}, f32[6,768]{1,0:T(8,128)}, f32[6,768]{1,0:T(8,128)}, f32[6,768]{1,0:T(8,128)}, /*index=5*/f32[6,768]{1,0:T(8,128)}, f32[6]{0:T(128)}) custom-call(bf16[256,768]{1,0:T(8,128)(2,1)} %get-tuple-element.21.refs_0_, bf16[256,768]{1,0:T(8,128)(2,1)} %get-tuple-element.22.refs_1_, ...), custom_call_target="tpu_custom_call" | custom-call | tf_op jit(solution)/shard_map/finish/pallas_call | solution.py:695

commit v4 on v3

--- a/solution.py
+++ b/solution.py
@@ -93,8 +93,8 @@
     x_hbm, u_hbm, gain_ref, wq_ref, wk_ref, wv_ref, we_ref,
     out_hbm, al_hbm, gq_ref, gk_ref, gv_ref, go_ref, dg_ref,
     x_ref, u_ref, out_ref, al_ref, n_all, wl, wr, wc, w_full, hot_s, sel_s, perm_g, perm_o,
-    q_s, k_s, v_s, a_s, kt_s, vt_s, a_out, a_in, lse_s, p_s, dp_s, dk_s, dv_s,
-    p_buf, b_buf, gt_s, rs, bc, acc1, bz, acc2, bx, acc3, finq, t_s,
+    q_s, k_s, v_s, a_s, kt_s, vt_s, a_out, a_in, e_s, r_s, p_s, dp_s, dk_s, dv_s,
+    p_buf, b_buf, gt_s, rs, bc, acc1, bz, acc3, finq, t_s,
     ro, boc, oc, boz, ox, box, oy, boy,
     ns, nr, ws, wrs, as_, ar, ps, pr, gs, gr, os_, or_, loc,
 ):
@@ -107,11 +107,13 @@
     z_peers = [at(d, xl * 8 + ((z + s) % 4) * 2 + core) for s in range(1, 4)]
     z_from = [((z + 4 - s) % 4) * 2 + core for s in range(1, 4)]
     c_peer = at(d, xl * 8 + z * 2 + 1 - core)
+    g0 = xl * 4 + z
+    g_peers = [at(d, 2 * ((g0 + s) % 8) + core) for s in range(1, 8)]
     x_in = pltpu.make_async_copy(x_hbm, x_ref, loc.at[3])
     u_in = pltpu.make_async_copy(u_hbm, u_ref, loc.at[4])
     x_in.start()
     u_in.start()
-    barrier(depth_peers + x_peers[1:] + z_peers + [c_peer])
+    barrier(depth_peers + x_peers[2:] + g_peers + [c_peer])
 
     top = jnp.concatenate(
         [wq_ref[...].astype(F32), wk_ref[...].astype(F32), wv_ref[0:4].astype(F32)], axis=0
@@ -299,7 +301,7 @@
             p_buf.at[c, rows], b_buf.at[c, rows], ps.at[kind, c], pr.at[kind, c], at(c, r)
         )
 
-    def forward(h, c):
+    def forward(h, c, k):
         q = q_s[h, pl.ds(pl.multiple_of(c * ROWS, ROWS), ROWS), :]
         m = jnp.full((8, ROWS), -jnp.inf, F32)
         for t in range(SEQ // TILE):
@@ -313,18 +315,21 @@
         for t in range(SEQ // TILE):
             e = jnp.exp(p_s[t * TILE:t * TILE + TILE, :] - m)
             l = l + jnp.sum(e.reshape(TILE // 8, 8, ROWS), axis=0)
-            att += dot(vt_s[h, t], e.astype(BF), 1, 0)
+            eb = e.astype(BF)
+            e_s[k, t * TILE:t * TILE + TILE, :] = eb
+            att += dot(vt_s[h, t], eb, 1, 0)
         l = jnp.sum(l, axis=0, keepdims=True)
-        p_buf[c, h * HD:h * HD + HD, :] = (att * (1.0 / l)).astype(BF)
-        lse_s[h, c] = m + jnp.log(l)
+        l = 1.0 / l
+        p_buf[c, h * HD:h * HD + HD, :] = (att * l).astype(BF)
+        r_s[k] = l
         pl.when(c != d)(lambda: sent(h, c).start())
 
     def forward_shared(i, _):
-        forward(1, 4 * par + i)
+        forward(1, 4 * par + i, 8 + i)
         return 0
 
     def forward_own(i, _):
-        forward(0, i)
+        forward(0, i, i)
         return 0
 
     lax.fori_loop(0, 4, forward_shared, 0)
@@ -348,25 +353,24 @@
         c.start()
         wc3.append(c)
 
-    def attend(h, c, base):
+    def attend(h, c, k, base):
         rows = pl.ds(pl.multiple_of(c * ROWS, ROWS), ROWS)
         q = q_s[h, rows, :]
         a = a_s[h, rows, :]
         qt, at_ = q.T, a.T
-        lse = lse_s[h, c]
+        scale = r_s[k]
         delta = jnp.zeros((8, ROWS), F32)
         for t in range(SEQ // TILE):
             ts = slice(t * TILE, t * TILE + TILE)
-            p = jnp.exp(dot(k_s[h, ts, :], q, 1, 1) - lse)
+            p = e_s[k, ts, :].astype(F32) * scale
             dp = dot(v_s[h, ts, :], a, 1, 1)
-            p_s[ts, :] = p
             dp_s[ts, :] = dp
             delta = delta + jnp.sum((p * dp).reshape(TILE // 8, 8, ROWS), axis=0)
         delta = jnp.sum(delta, axis=0, keepdims=True)
         dq = jnp.zeros((HD, ROWS), F32)
         for t in range(SEQ // TILE):
             ts = slice(t * TILE, t * TILE + TILE)
-            p = p_s[ts, :]
+            p = e_s[k, ts, :].astype(F32) * scale
             pb = p.astype(BF)
             ds = (p * (dp_s[ts, :] - delta)).astype(BF)
             dq += dot(kt_s[h, t], ds, 1, 0)
@@ -384,12 +388,12 @@
 
     def attend_shared(i, _):
         c = 4 * par + i
-        attend(1, c, 448)
+        attend(1, c, 8 + i, 448)
         pl.when(c != d)(lambda: sent(5, c).start())
         return 0
 
     def attend_own(c, _):
-        attend(0, c, 128)
+        attend(0, c, c, 128)
         pl.when(c != d)(lambda: sent(2, c).start())
         return 0
 
@@ -404,35 +408,30 @@
         for b in range(2):
             rs[h, b] = moved(perm_g[b].reshape(512, E), gt_s[...], 1, 1).reshape(8, 64, 192)
 
+    def to_core(h):
+        out = [
+            remote(rs.at[h, 1 - core, g], bc.at[h, g], gs.at[h, g], gr.at[h, g], c_peer) for g in range(8)
+        ]
+        start(out)
+        return out
+
     def sum_cores(h, copies):
         for g in range(8):
             copies[g].wait()
             acc1[h, g] = (rs[h, core, g].astype(F32) + bc[h, g].astype(F32)).astype(BF)
         out = []
-        for s in range(1, 4):
-            for q in range(2):
-                k = 8 + (s - 1) * 2 + q
-                to = acc1.at[h, q * 4 + (z + s) % 4]
-                out.append(remote(to, bz.at[h, s - 1, q], gs.at[h, k], gr.at[h, k], z_peers[s - 1]))
+        for s in range(1, 8):
+            to = (g0 + s) % 8
+            out.append(remote(acc1.at[h, to], bz.at[h, g0], gs.at[h, 7 + s], gr.at[h, 7 + s], g_peers[s - 1]))
         start(out)
         return out
 
-    def sum_z(h, copies):
+    def sum_up(h, copies):
         wait(copies)
-        for q in range(2):
-            acc2[h, q] = (
-                acc1[h, q * 4 + z].astype(F32)
-                + bz[h, 0, q].astype(F32)
-                + bz[h, 1, q].astype(F32)
-                + bz[h, 2, q].astype(F32)
-            ).astype(BF)
-        out = remote(acc2.at[h, 1 - xl], bx.at[h], gs.at[h, 14], gr.at[h, 14], x_peers[1])
-        out.start()
-        return out
-
-    def sum_x(h, copy):
-        copy.wait()
-        acc3[h] = acc2[h, xl].astype(F32) + bx[h].astype(F32)
+        total = acc1[h, g0].astype(F32)
+        for s in range(1, 8):
+            total += bz[h, (g0 + s) % 8].astype(F32)
+        acc3[h] = total
         out = []
         for s in range(1, ND):
             rows = pl.ds(pl.multiple_of(((d + s) % ND) * 8, 8), 8)
@@ -448,10 +447,7 @@
     lax.fori_loop(0, 4, attend_shared, 0)
     totals(320, 4)
     grads(1)
-    sc = [
-        remote(rs.at[1, 1 - core, g], bc.at[1, g], gs.at[1, g], gr.at[1, g], c_peer) for g in range(8)
-    ]
-    start(sc)
+    sc = to_core(1)
 
     local.wait()
     for s in range(1, ND):
@@ -501,7 +497,6 @@
         remote(ox.at[x_to[s]], box.at[s], os_.at[7 + s], or_.at[7 + s], x_peers[s]) for s in range(3)
     ]
     start(ox_copies)
-    sx = sum_z(1, sz)
     lax.fori_loop(5, 7, attend_own, 0)
     wait(ox_copies)
     total = (
@@ -514,17 +509,14 @@
         for s in range(1, 4)
     ]
     start(oy_copies)
-    sd = sum_x(1, sx)
+    sd = sum_up(1, sz)
     lax.fori_loop(7, 8, attend_own, 0)
     totals(192, 3)
     local = pltpu.make_async_copy(p_buf.at[d, 128:512], b_buf.at[d, 128:512], loc.at[2])
     local.start()
 
     grads(0)
-    cc = [
-        remote(rs.at[0, 1 - core, g], bc.at[0, g], gs.at[0, g], gr.at[0, g], c_peer) for g in range(8)
-    ]
-    start(cc)
+    cc = to_core(0)
 
     wait(wc3)
     for g in range(8):
@@ -539,30 +531,34 @@
 
     cz = sum_cores(0, cc)
 
-    local.wait()
     for s in range(1, ND):
         c = (d + s) % ND
-        for kind in (2, 3, 4):
+        came(2, c).wait_recv()
+        pl.when(c % 2 == half)(came(5, c).wait_recv)
+    local.wait()
+    for k in range(4):
+        t_s[1, 192 * k:192 * k + 64] = b_buf[2 * k, 128:192]
+        t_s[1, 192 * k + 64:192 * k + 128] = b_buf[2 * k + half, 448:512]
+        t_s[1, 192 * k + 128:192 * k + 192] = b_buf[2 * k + 1, 128:192]
+    dn = dot(t_s[1].T, w_full[0], 1, 1)
+    last = sum_up(0, cz)
+
+    for s in range(1, ND):
+        c = (d + s) % ND
+        for kind in (3, 4):
             came(kind, c).wait_recv()
-        pl.when(c % 2 == half)(came(5, c).wait_recv)
     for k in range(4):
         lo, hi = 2 * k, 2 * k + 1
-        for m in range(3):
-            rows = slice(128 + 64 * m, 192 + 64 * m)
-            t_s[1 + m, 192 * k:192 * k + 64] = b_buf[lo, rows]
-            t_s[1 + m, 192 * k + 128:192 * k + 192] = b_buf[hi, rows]
-        t_s[1, 192 * k + 64:192 * k + 128] = b_buf[lo + half, 448:512]
         for m in range(2):
+            rows = slice(192 + 64 * m, 256 + 64 * m)
+            t_s[2 + m, 192 * k:192 * k + 64] = b_buf[lo, rows]
+            t_s[2 + m, 192 * k + 128:192 * k + 192] = b_buf[hi, rows]
             rows = slice(320 + 64 * m, 384 + 64 * m)
             t_s[2 + m, 192 * k + 64:192 * k + 128] = (
                 b_buf[lo, rows].astype(F32) + b_buf[hi, rows].astype(F32)
             ).astype(BF)
-
-    cx = sum_z(0, cz)
-    dn = dot(t_s[1].T, w_full[0], 1, 1)
     dn += dot(t_s[2].T, w_full[1], 1, 1)
     dn += dot(t_s[3].T, w_full[2], 1, 1)
-    last = sum_x(0, cx)
     x = x_ref[...].astype(F32)
     centered = x - jnp.mean(x, axis=-1, keepdims=True)
     inverse = lax.rsqrt(jnp.mean(centered * centered, axis=-1, keepdims=True) + 1e-05)
@@ -649,7 +645,8 @@
             pltpu.VMEM((2, ND, HD, ROWS), BF),
             pltpu.VMEM((ND, ROWS, 128), BF),
             pltpu.VMEM((ND, ROWS, 128), BF),
-            pltpu.VMEM((2, ND, 1, ROWS), F32),
+            pltpu.VMEM((12, SEQ, ROWS), BF),
+            pltpu.VMEM((12, 1, ROWS), F32),
             pltpu.VMEM((SEQ, ROWS), F32),
             pltpu.VMEM((SEQ, ROWS), F32),
             pltpu.VMEM((HD, SEQ), F32),
@@ -660,9 +657,7 @@
             pltpu.VMEM((2, 2, 8, 64, 192), BF),
             pltpu.VMEM((2, 8, 64, 192), BF),
             pltpu.VMEM((2, 8, 64, 192), BF),
-            pltpu.VMEM((2, 3, 2, 64, 192), BF),
-            pltpu.VMEM((2, 2, 64, 192), BF),
-            pltpu.VMEM((2, 64, 192), BF),
+            pltpu.VMEM((2, 8, 64, 192), BF),
             pltpu.VMEM((2, 64, 192), F32),
             pltpu.VMEM((2, ND, 8, 192), F32),
             pltpu.VMEM((4, E, ROWS), BF),

time: 118 us -> 114 us (0.966)
  Pallas kernels: 118 us -> 113 us
    pallas_call x1, Pallas kernels: 116 us -> 111 us  [fused(): pl.pallas_call(kernel, out_shape=(jax.ShapeDtypeStruct((ROWS, E), BF), ja...]
where the time goes in v4:
time: 114 us
  Pallas kernels  113 us (99%)
    pallas_call x1, Pallas kernels, fused(): pl.pallas_call(kernel, out_shape=(jax.ShapeDtypeStruct((ROWS, E), BF), ja...  111 us

profile of v4, /device:TPU:0, one launch (start us, length us, event | category | flops | bytes accessed | tf_op | source)
XLA Modules:
  0.0 113.5 jit_solution(7246789725552106450)
XLA Ops:
  0.6 110.8 %fused.1 = (bf16[256,768]{1,0:T(8,128)(2,1)}, bf16[256,768]{1,0:T(8,128)(2,1)}, f32[6,768]{1,0:T(8,128)}, f32[6,768]{1,0:T(8,128)}, f32[6,768]{1,0:T(8,128)}, /*index=5*/f32[6,768]{1,0:T(8,128)}, f32[8,128]{1,0:T(8,128)}) custom-call(bf16[256,768]{1,0:T(8,128)(2,1)} %bitcast.4, bf16[256,768]{1,0:T(8,128)(2,1)} %bitcast.5, f32[768]{0:T(1024)} %gain_ref.1, ...), custom_call_target="tpu_custom_call" | custom-call | tf_op jit(solution)/shard_map/fused/pallas_call | solution.py:616
  111.4 2.1 %finish.1 = (bf16[256,768]{1,0:T(8,128)(2,1)}, bf16[256,768]{1,0:T(8,128)(2,1)}, f32[6,768]{1,0:T(8,128)}, f32[6,768]{1,0:T(8,128)}, f32[6,768]{1,0:T(8,128)}, /*index=5*/f32[6,768]{1,0:T(8,128)}, f32[6]{0:T(128)}) custom-call(bf16[256,768]{1,0:T(8,128)(2,1)} %get-tuple-element.21.refs_0_, bf16[256,768]{1,0:T(8,128)(2,1)} %get-tuple-element.22.refs_1_, ...), custom_call_target="tpu_custom_call" | custom-call | tf_op jit(solution)/shard_map/finish/pallas_call | solution.py:690

commit v5 on v4

--- a/solution.py
+++ b/solution.py
@@ -314,8 +314,8 @@
         att = jnp.zeros((HD, ROWS), F32)
         for t in range(SEQ // TILE):
             e = jnp.exp(p_s[t * TILE:t * TILE + TILE, :] - m)
-            l = l + jnp.sum(e.reshape(TILE // 8, 8, ROWS), axis=0)
             eb = e.astype(BF)
+            l = l + jnp.sum(eb.astype(F32).reshape(TILE // 8, 8, ROWS), axis=0)
             e_s[k, t * TILE:t * TILE + TILE, :] = eb
             att += dot(vt_s[h, t], eb, 1, 0)
         l = jnp.sum(l, axis=0, keepdims=True)

time: 114 us -> 114 us (level)
  no operation moved by 1% of the time
where the time goes in v5:
time: 114 us
  Pallas kernels  114 us (100%)
    pallas_call x1, Pallas kernels, fused(): pl.pallas_call(kernel, out_shape=(jax.ShapeDtypeStruct((ROWS, E), BF), ja...  112 us

profile of v5, /device:TPU:0, one launch (start us, length us, event | category | flops | bytes accessed | tf_op | source)
XLA Modules:
  0.0 114.3 jit_solution(2261370739399357687)
XLA Ops:
  0.6 111.6 %fused.1 = (bf16[256,768]{1,0:T(8,128)(2,1)}, bf16[256,768]{1,0:T(8,128)(2,1)}, f32[6,768]{1,0:T(8,128)}, f32[6,768]{1,0:T(8,128)}, f32[6,768]{1,0:T(8,128)}, /*index=5*/f32[6,768]{1,0:T(8,128)}, f32[8,128]{1,0:T(8,128)}) custom-call(bf16[256,768]{1,0:T(8,128)(2,1)} %bitcast.4, bf16[256,768]{1,0:T(8,128)(2,1)} %bitcast.5, f32[768]{0:T(1024)} %gain_ref.1, ...), custom_call_target="tpu_custom_call" | custom-call | tf_op jit(solution)/shard_map/fused/pallas_call | solution.py:616
  112.2 2.1 %finish.1 = (bf16[256,768]{1,0:T(8,128)(2,1)}, bf16[256,768]{1,0:T(8,128)(2,1)}, f32[6,768]{1,0:T(8,128)}, f32[6,768]{1,0:T(8,128)}, f32[6,768]{1,0:T(8,128)}, /*index=5*/f32[6,768]{1,0:T(8,128)}, f32[6]{0:T(128)}) custom-call(bf16[256,768]{1,0:T(8,128)(2,1)} %get-tuple-element.21.refs_0_, bf16[256,768]{1,0:T(8,128)(2,1)} %get-tuple-element.22.refs_1_, ...), custom_call_target="tpu_custom_call" | custom-call | tf_op jit(solution)/shard_map/finish/pallas_call | solution.py:690
